TPU v7x, 768 devices: a whole 4x8x12 slice. The times are simulated.
768 devices in a mesh: dp: 8 (over y_hi, core), ctx: 8 (over y_lo, x), tp: 12 (over z).
Axes of the slice: x: 4, y: 8 (y_hi: 4, y_lo: 2; y = y_hi * 2 + y_lo), z: 12, core: 2. Of those that a mesh axis runs over, the one named last changes fastest.
Arguments:
- grad_out: bfloat16 [64, 24, 4096], P(('dp', 'ctx'), 'tp'), may hold values from -6 to 6
- probs: bfloat16 [64, 24, 8], P(('dp', 'ctx')), may hold values from 0.099609375 to 1
- expert_ids: int32 [64, 24, 8], P(('dp', 'ctx')), may hold values from 0 to 63, all different within a row; in each aligned block of 24 rows (0 to 23, 24 to 47, ..., all dimensions but the last counted through in order) at most 4 rows name the same one
- saved_inputs: bfloat16 [64, 64, 4, 4096], P(('dp', 'ctx')), may hold values from -6 to 6
- w_gate: bfloat16 [64, 4096, 768], P(('dp', 'ctx'), None, 'tp'), may hold values from -0.09375 to 0.09375
- w_up: bfloat16 [64, 4096, 768], P(('dp', 'ctx'), None, 'tp'), may hold values from -0.09375 to 0.09375
- w_down: bfloat16 [64, 768, 4096], P(('dp', 'ctx'), 'tp'), may hold values from -0.046875 to 0.046875
Outputs:
- grad_tokens: bfloat16 [64, 24, 4096], P(('dp', 'ctx'), 'tp')
- grad_probs: float32 [64, 24, 8], P(('dp', 'ctx'), 'tp')
- grad_gate: bfloat16 [64, 4096, 768], P(('dp', 'ctx'), None, 'tp')
- grad_up: bfloat16 [64, 4096, 768], P(('dp', 'ctx'), None, 'tp')
- grad_down: bfloat16 [64, 768, 4096], P(('dp', 'ctx'), 'tp')
Inputs may be any that keep to these rules, and one draw needn't show every extreme that they name: `expert_ids`: each row names 8 different experts. Within one index of the first dimension no expert is named by more than 4 rows, a bound that some block reaches.
All inputs are finite; a program needn't handle non-finite values.
Results may differ from a plain program's by a relative error of at most 0.0065.
Values may be sent and summed in bfloat16 or wider, within the bound.
No kernel may reach another device: no remote copies, remote signals or barrier semaphores. Data moves between devices by JAX's collectives and lax.ppermute only.
A program may use at most 32 MiB of HBM per device.

v0:
```python
import jax
import jax.numpy as jnp
from jax import lax
from jax.sharding import PartitionSpec as P


def slot_index(routes, experts, capacity):
    flattened = routes.reshape(-1)
    onehot = (flattened[:, None] == jnp.arange(experts, dtype=jnp.int32)[None, :]).astype(jnp.int32)
    before = jnp.cumsum(onehot, axis=0) - onehot
    ranking = jnp.sum(before * onehot, axis=1)
    return (flattened * capacity + ranking).reshape(routes.shape)


def chooser_table(slots, slot_count):
    return (slots[None, :, :] == jnp.arange(slot_count, dtype=jnp.int32)[:, None, None]).astype(
        jnp.float32
    )


def expert_terms(rows_input, rows_grad, rows_weight, gate_slice, up_slice, down_slice):
    gate_pre = jnp.dot(rows_input, gate_slice, preferred_element_type=jnp.float32)
    up_pre = jnp.dot(rows_input, up_slice, preferred_element_type=jnp.float32)
    sigmoid_gate = jax.nn.sigmoid(gate_pre)
    activated = gate_pre * sigmoid_gate
    hidden = activated * up_pre
    upward = lax.dot_general(
        rows_grad, down_slice, (((1,), (1,)), ((), ())), preferred_element_type=jnp.float32
    )
    part_prob = jnp.sum(hidden * upward, axis=1).astype(jnp.bfloat16)
    weight_col = rows_weight.astype(jnp.float32)[:, None]
    hidden_grad = weight_col * upward
    gate_grad = (
        hidden_grad * up_pre * sigmoid_gate * (1.0 + gate_pre * (1.0 - sigmoid_gate))
    ).astype(jnp.bfloat16)
    up_grad = (hidden_grad * activated).astype(jnp.bfloat16)
    part_grad = lax.dot_general(
        gate_grad, gate_slice, (((1,), (1,)), ((), ())), preferred_element_type=jnp.float32
    )
    part_grad = part_grad + lax.dot_general(
        up_grad, up_slice, (((1,), (1,)), ((), ())), preferred_element_type=jnp.float32
    )
    part_grad = part_grad.astype(jnp.bfloat16)
    scaled = (weight_col * rows_grad.astype(jnp.float32)).astype(jnp.bfloat16)
    grad_down = lax.dot_general(
        hidden.astype(jnp.bfloat16),
        scaled,
        (((0,), (0,)), ((), ())),
        preferred_element_type=jnp.float32,
    ).astype(jnp.bfloat16)
    grad_gate = lax.dot_general(
        rows_input, gate_grad, (((0,), (0,)), ((), ())), preferred_element_type=jnp.float32
    ).astype(jnp.bfloat16)
    grad_up = lax.dot_general(
        rows_input, up_grad, (((0,), (0,)), ((), ())), preferred_element_type=jnp.float32
    ).astype(jnp.bfloat16)
    return (part_grad, part_prob, grad_gate, grad_up, grad_down)


def body(grad_out, probs, expert_ids, saved_inputs, w_gate, w_up, w_down):
    column = lax.all_gather(grad_out, "tp", axis=1, tiled=True)[0]
    dp_count = lax.axis_size("dp")
    ctx_count = lax.axis_size("ctx")
    expert_count = dp_count * ctx_count
    capacity = saved_inputs.shape[2]
    model_width = column.shape[1]
    slot_count = expert_count * capacity
    chooser = chooser_table(slot_index(expert_ids[0], expert_count, capacity), slot_count)
    picker = jnp.sum(chooser, axis=2).astype(jnp.bfloat16)
    sent_grad = jnp.dot(picker, column, preferred_element_type=jnp.float32).astype(jnp.bfloat16)
    sent_weight = jnp.einsum("sjk,jk->s", chooser, probs[0].astype(jnp.float32)).astype(
        jnp.bfloat16
    )
    got_grad, got_weight = (
        lax.all_to_all(
            sent_grad.reshape(expert_count, capacity, model_width),
            ("dp", "ctx"),
            split_axis=0,
            concat_axis=0,
            tiled=True,
        ),
        lax.all_to_all(
            sent_weight.reshape(expert_count, capacity),
            ("dp", "ctx"),
            split_axis=0,
            concat_axis=0,
            tiled=True,
        ),
    )
    part_grad, part_prob, grad_gate, grad_up, grad_down = expert_terms(
        saved_inputs[0].reshape(slot_count, model_width),
        got_grad.reshape(slot_count, model_width),
        got_weight.reshape(slot_count),
        w_gate[0],
        w_up[0],
        w_down[0],
    )
    back_grad, back_prob = (
        lax.all_to_all(
            part_grad.reshape(expert_count, capacity, model_width),
            ("dp", "ctx"),
            split_axis=0,
            concat_axis=0,
            tiled=True,
        ),
        lax.all_to_all(
            part_prob.reshape(expert_count, capacity),
            ("dp", "ctx"),
            split_axis=0,
            concat_axis=0,
            tiled=True,
        ),
    )
    token_grad_sum = lax.dot_general(
        picker,
        back_grad.reshape(slot_count, model_width),
        (((0,), (0,)), ((), ())),
        preferred_element_type=jnp.float32,
    )
    weight_grad_sum = jnp.einsum(
        "sjk,s->jk", chooser, back_prob.reshape(slot_count).astype(jnp.float32)
    )
    grad_tokens, grad_probs = (
        lax.psum_scatter(token_grad_sum, "tp", scatter_dimension=0, tiled=True),
        lax.psum_scatter(weight_grad_sum, "tp", scatter_dimension=0, tiled=True),
    )
    return (
        grad_tokens.astype(jnp.bfloat16)[None],
        grad_probs[None],
        grad_gate[None],
        grad_up[None],
        grad_down[None],
    )


def solution(mesh):
    placed = (
        P(("dp", "ctx"), "tp", None),
        P(("dp", "ctx"), None, None),
        P(("dp", "ctx"), None, None),
        P(("dp", "ctx"), None, None, None),
        P(("dp", "ctx"), None, "tp"),
        P(("dp", "ctx"), None, "tp"),
        P(("dp", "ctx"), "tp", None),
    )
    return jax.shard_map(
        body,
        mesh=mesh,
        in_specs=placed,
        out_specs=(
            P(("dp", "ctx"), "tp", None),
            P(("dp", "ctx"), "tp", None),
            P(("dp", "ctx"), None, "tp"),
            P(("dp", "ctx"), None, "tp"),
            P(("dp", "ctx"), "tp", None),
        ),
        check_vma=False,
    )
```

profile of v0, /device:TPU:2, one launch (start us, length us, event | category | flops | bytes accessed | tf_op | source)
XLA Modules:
  0.0 245.4 jit_solution(3253927396176303545)
XLA Ops:
  0.6 0.0 copy-start
  0.6 0.8 copy.31
  1.5 0.1 eq.37
  1.6 0.8 copy.38
  2.4 0.6 reduce-window.6
  3.0 0.2 slice_reduce_fusion
  3.2 0.1 bitcast_bitcast_fusion
  3.3 0.1 reduce_sum.30
  3.4 0.2 fusion.17
  3.7 0.7 all_to_all.21
  4.4 13.6 %all-to-all-start = ((bf16[64,1,4]{2,1,0:T(2,128)(2,1)}), bf16[64,1,4]{2,1,0:T(2,128)(2,1)S(1)}, u32[]{:S(2)}, u32[]{:S(2)}) async-start(bf16[64,1,4]{2,1,0:T(2,128)(2,1)} %all_to_all.21), calls=%async_computation | async-start | bytes 65536 | tf_op jit(solution)/shard_map/all_to_all | solution.py:82
  18.0 0.1 convert_reduce_fusion
  18.1 0.7 copy.36
  18.9 31.6 %all_gather.3 = bf16[1,24,4096]{2,0,1:T(2,128)(2,1)S(1)} all-gather(bf16[1,2,4096]{2,0,1:T(2,128)(2,1)S(1)} %copy.36), channel_id=1, replica_groups=mesh['dp'=8,'ctx'=8,'tp'=12] {'tp'}, dimensions={1}, use_global_device_ids=true | all-gather | bytes 212992 | tf_op jit(solution)/shard_map/all_gather | solution.py:61
  50.5 0.7 convolution_convert_fusion
  51.2 2.2 reshape.69
  53.5 0.0 all-to-all-done
  53.5 10.5 %all-to-all-start.1 = ((bf16[64,4,4096]{2,1,0:T(4,128)(2,1)}), bf16[64,4,4096]{2,1,0:T(4,128)(2,1)}, u32[]{:S(2)}, u32[]{:S(2)}) async-start(bf16[64,4,4096]{2,1,0:T(4,128)(2,1)} %reshape.69), calls=%async_computation.1 | async-start | bytes 4194304 | tf_op jit(solution)/shard_map/all_to_all | solution.py:75
  64.0 2.5 %reshape_squeeze.4 = bf16[256,4096]{1,0:T(8,128)(2,1)S(1)} reshape(bf16[1,64,4,4096]{3,2,1,0:T(4,128)(2,1)} %param.10) | data formatting | bytes 4194304 | tf_op jit(solution)/shard_map/reshape;squeeze | solution.py:91
  66.6 0.0 copy-done
  66.6 0.0 copy-start.2
  66.6 0.8 fusion.7
  67.4 0.3 copy-done.2
  67.7 0.8 fusion.10
  68.4 0.1 convert_reduce_fusion.1
  68.5 0.1 reshape.75
  68.6 46.6 %all-to-all-done.1 = bf16[64,4,4096]{2,1,0:T(4,128)(2,1)} async-done(((bf16[64,4,4096]{2,1,0:T(4,128)(2,1)}), bf16[64,4,4096]{2,1,0:T(4,128)(2,1)}, u32[]{:S(2)}, u32[]{:S(2)}) %all-to-all-start.1) | async-done | bytes 2097184 | tf_op jit(solution)/shard_map/all_to_all | solution.py:75
  115.2 4.0 %reshape.70 = bf16[256,4096]{1,0:T(8,128)(2,1)} reshape(bf16[64,4,4096]{2,1,0:T(4,128)(2,1)} %all-to-all-done.1) | data formatting | bytes 4194304 | tf_op jit(solution)/shard_map/reshape | solution.py:92
  119.2 2.5 %multiply_reduce_fusion = (bf16[256]{0:T(256)(128)(2,1)S(1)}, bf16[256,64]{0,1:T(8,128)(2,1)S(1)}, bf16[256,64]{0,1:T(8,128)(2,1)S(1)}) fusion(f32[256,64]{0,1:T(8,128)S(1)} %fusion.10, f32[256,64]{0,1:T(8,128)S(1)} %fusion.7, f32[256]{0:T(256)S(1)} %reshape.75, bf16[256,4096]{1,0:T(8,128)(2,1)} %reshape.70, bf16[1,64,4096]{2,1,0:T(8,128)(2,1)} %param.13), kind=kOutput, calls=%fused_computation.35 | convolution fusion | flops 134496000 | bytes 2819584 | tf_op jit(solution)/shard_map/dot_general | solution.py:27
  121.6 0.7 convert_element_type.100
  122.4 5.5 %all-to-all-start.3 = ((bf16[64,1,4]{2,1,0:T(2,128)(2,1)}), bf16[64,1,4]{2,1,0:T(2,128)(2,1)S(1)}, u32[]{:S(2)}, u32[]{:S(2)}) async-start(bf16[64,1,4]{2,1,0:T(2,128)(2,1)} %convert_element_type.100), calls=%async_computation.3 | async-start | bytes 65536 | tf_op jit(solution)/shard_map/all_to_all | solution.py:106
  127.9 0.7 fusion.5
  128.7 2.1 fusion
  130.7 4.1 %reshape.71 = bf16[64,4,4096]{2,1,0:T(4,128)(2,1)} reshape(bf16[256,4096]{1,0:T(8,128)(2,1)} %fusion) | data formatting | bytes 4194304 | tf_op jit(solution)/shard_map/reshape | solution.py:100
  134.8 1.6 all-to-all-done.3
  136.5 8.8 %all-to-all-start.2 = ((bf16[64,4,4096]{2,1,0:T(4,128)(2,1)}), bf16[64,4,4096]{2,1,0:T(4,128)(2,1)}, u32[]{:S(2)}, u32[]{:S(2)}) async-start(bf16[64,4,4096]{2,1,0:T(4,128)(2,1)} %reshape.71), calls=%async_computation.2 | async-start | bytes 4194304 | tf_op jit(solution)/shard_map/all_to_all | solution.py:99
  145.3 1.3 dynamic-slice
  147.2 0.0 copy-start.1
  147.3 1.3 fusion.1
  148.5 1.3 fusion.2
  149.8 0.0 copy-done.1
  149.8 1.4 fusion.3
  151.2 0.1 reduce.2
  151.3 0.1 reshape.78
  151.5 0.4 fusion.16
  151.8 44.6 %all-to-all-done.2 = bf16[64,4,4096]{2,1,0:T(4,128)(2,1)} async-done(((bf16[64,4,4096]{2,1,0:T(4,128)(2,1)}), bf16[64,4,4096]{2,1,0:T(4,128)(2,1)}, u32[]{:S(2)}, u32[]{:S(2)}) %all-to-all-start.2) | async-done | bytes 2097184 | tf_op jit(solution)/shard_map/all_to_all | solution.py:99
  196.5 2.5 %reshape.72 = bf16[256,4096]{1,0:T(8,128)(2,1)S(1)} reshape(bf16[64,4,4096]{2,1,0:T(4,128)(2,1)} %all-to-all-done.2) | data formatting | bytes 4194304 | tf_op jit(solution)/shard_map/reshape | solution.py:116
  199.0 0.4 fusion.30
  199.4 44.7 %all-reduce.5 = (bf16[24,4096]{1,0:T(8,128)(2,1)S(1)}, f32[24,8]{1,0:T(8,128)S(1)}) all-reduce(f32[24,4096]{1,0:T(8,128)S(1)} %fusion.30, f32[24,8]{1,0:T(8,128)S(1)} %bitcast.66), channel_id=2, replica_groups=mesh['dp'=8,'ctx'=8,'tp'=12] {'tp'}, use_global_device_ids=true, to_apply=%region_4.5.clone | all-reduce | flops 98496 | bytes 591360
  244.2 0.6 fusion.25
  244.8 0.6 dynamic-slice_bitcast_fusion
  (7 shorter events, 0.1 us)
Async XLA Ops:
  0.6 66.0 %copy-start = (bf16[1,4096,64]{1,2,0:T(8,128)(2,1)S(1)}, bf16[1,4096,64]{1,2,0:T(8,128)(2,1)}, u32[]{:S(2)}) copy-start(bf16[1,4096,64]{1,2,0:T(8,128)(2,1)} %param.11) | copy-start | bytes 1572868
  4.4 49.1 %all-to-all-start = ((bf16[64,1,4]{2,1,0:T(2,128)(2,1)}), bf16[64,1,4]{2,1,0:T(2,128)(2,1)S(1)}, u32[]{:S(2)}, u32[]{:S(2)}) async-start(bf16[64,1,4]{2,1,0:T(2,128)(2,1)} %all_to_all.21), calls=%async_computation | async-start | bytes 65536 | tf_op jit(solution)/shard_map/all_to_all | solution.py:82
  53.5 61.7 %all-to-all-start.1 = ((bf16[64,4,4096]{2,1,0:T(4,128)(2,1)}), bf16[64,4,4096]{2,1,0:T(4,128)(2,1)}, u32[]{:S(2)}, u32[]{:S(2)}) async-start(bf16[64,4,4096]{2,1,0:T(4,128)(2,1)} %reshape.69), calls=%async_computation.1 | async-start | bytes 4194304 | tf_op jit(solution)/shard_map/all_to_all | solution.py:75
  66.6 1.0 copy-start.2
  122.4 14.1 %all-to-all-start.3 = ((bf16[64,1,4]{2,1,0:T(2,128)(2,1)}), bf16[64,1,4]{2,1,0:T(2,128)(2,1)S(1)}, u32[]{:S(2)}, u32[]{:S(2)}) async-start(bf16[64,1,4]{2,1,0:T(2,128)(2,1)} %convert_element_type.100), calls=%async_computation.3 | async-start | bytes 65536 | tf_op jit(solution)/shard_map/all_to_all | solution.py:106
  136.5 60.0 %all-to-all-start.2 = ((bf16[64,4,4096]{2,1,0:T(4,128)(2,1)}), bf16[64,4,4096]{2,1,0:T(4,128)(2,1)}, u32[]{:S(2)}, u32[]{:S(2)}) async-start(bf16[64,4,4096]{2,1,0:T(4,128)(2,1)} %reshape.71), calls=%async_computation.2 | async-start | bytes 4194304 | tf_op jit(solution)/shard_map/all_to_all | solution.py:99
  147.2 2.6 %copy-start.1 = (bf16[256,4096]{1,0:T(8,128)(2,1)S(1)}, bf16[256,4096]{1,0:T(8,128)(2,1)}, u32[]{:S(2)}) copy-start(bf16[256,4096]{1,0:T(8,128)(2,1)} %reshape.70) | copy-start | bytes 6291460
where the time goes:
time: 246 us; the launch traced here: 245 us
  waiting for transfers between devices  92.9 us (38%)
  blocking collectives  76.3 us (31%)
  starting transfers between devices  38.5 us (16%)
  local copies, waits for them, and re-layouts  22.6 us (9%)
  matrix products  12.5 us (5%)
    all_to_all x1, waiting for transfers between devices, body(): lax.all_to_all(sent_grad.reshape(expert_count, capacity, model_width), ('...  46.6 us
    unnamed x1, blocking collectives  44.7 us
    all_to_all x1, waiting for transfers between devices, body(): lax.all_to_all(part_grad.reshape(expert_count, capacity, model_width), ('...  44.6 us
    all_gather x1, blocking collectives, body(): column = lax.all_gather(grad_out, 'tp', axis=1, tiled=True)[0]  31.6 us
    all_to_all x1, starting transfers between devices, body(): lax.all_to_all(sent_weight.reshape(expert_count, capacity), ('dp', 'ctx')...  13.6 us
    all_to_all x1, starting transfers between devices, body(): lax.all_to_all(sent_grad.reshape(expert_count, capacity, model_width), ('...  10.5 us
    all_to_all x1, starting transfers between devices, body(): lax.all_to_all(part_grad.reshape(expert_count, capacity, model_width), ('...  8.82 us
    all_to_all x1, starting transfers between devices, body(): lax.all_to_all(part_prob.reshape(expert_count, capacity), ('dp', 'ctx'),...  5.52 us
  transfers between devices with their start and end apart: 4, of which 3 were waited for; matrix products, arithmetic and copies ran while one was open for 9% of the time, Pallas kernels for 0%

commit v1 on v0

v1 whole, which is shorter than its diff:
```python
import jax
import jax.numpy as jnp
from jax import lax
from jax.experimental import pallas as pl
from jax.experimental.pallas import tpu as pltpu
from jax.sharding import PartitionSpec as P

PARTS = 3
LANES = 128
F32, BF16 = jnp.float32, jnp.bfloat16
COLUMN = ("dp", "ctx")
VMEM = pl.BlockSpec(memory_space=pltpu.VMEM)
SMEM = pl.BlockSpec(memory_space=pltpu.SMEM)


def call(kernel, outs, in_specs, flops, bytes_accessed, scratch=()):
    return pl.pallas_call(
        kernel,
        out_shape=outs,
        in_specs=in_specs,
        out_specs=jax.tree.map(lambda _: VMEM, outs),
        scratch_shapes=scratch,
        compiler_params=pltpu.CompilerParams(vmem_limit_bytes=40 << 20),
        cost_estimate=pl.CostEstimate(
            flops=flops, bytes_accessed=bytes_accessed, transcendentals=0
        ),
    )


def route_kernel(cap, ids_ref, probs_ref, pick_ref, back_ref):
    top, tokens = ids_ref.shape
    slots, width = pick_ref.shape
    row = lax.broadcasted_iota(jnp.int32, (slots, tokens), 0)
    expert, place = row // cap, row % cap
    ids = ids_ref[...]
    probs = probs_ref[...].astype(F32)
    member = jnp.zeros((slots, tokens), F32)
    weight = jnp.zeros((slots, tokens), F32)
    for k in range(top):
        same = expert == ids[k : k + 1, :]
        member = jnp.where(same, 1.0, member)
        weight = jnp.where(same, probs[k : k + 1, :], weight)
    before = lax.broadcasted_iota(jnp.int32, (tokens, tokens), 0) < lax.broadcasted_iota(
        jnp.int32, (tokens, tokens), 1
    )
    rank = jnp.dot(
        member.astype(BF16), before.astype(F32).astype(BF16), preferred_element_type=F32
    )
    pick = jnp.where(rank == place.astype(F32), member, 0.0)
    slot_weight = jnp.sum(pick * weight, axis=1, keepdims=True)
    tail = lax.broadcasted_iota(jnp.int32, (slots, width - tokens), 1)
    full = jnp.concatenate([pick, jnp.where(tail == 0, slot_weight, 0.0)], axis=1)
    pick_ref[...] = full.astype(BF16)
    back_ref[...] = full.T.astype(BF16)


def send_kernel(part_ref, pick_ref, column_ref, out_ref):
    peers, own, width = column_ref.shape
    tokens = peers * own
    experts, cap, _ = out_ref.shape
    column = column_ref[...].astype(F32).reshape(tokens, width)
    rest = pick_ref.shape[1] - tokens
    lane = lax.broadcasted_iota(jnp.int32, (rest, width), 1)
    deep = lax.broadcasted_iota(jnp.int32, (rest, width), 0)
    padded = (deep == 0) & (lane >= width - LANES) & (part_ref[0] == PARTS - 1)
    column = jnp.concatenate([column, padded.astype(F32)], axis=0).astype(BF16)
    rows = jnp.dot(pick_ref[...], column, preferred_element_type=F32)
    out_ref[...] = rows.reshape(experts, cap, width).astype(BF16)


def expert_kernel(
    part_ref, mine_ref, low_ref, high_ref, gate_ref, up_ref, w_gate_ref, w_up_ref, w_down_ref,
    own_ref, to_high_ref, to_low_ref, rows_ref, gate_grad_ref, up_grad_ref, hidden_ref,
    stage_ref,
):
    experts, cap, width = mine_ref.shape
    slots = experts * cap
    model = w_down_ref.shape[1]
    part = part_ref[0]
    above, below = lax.rem(part + 1, PARTS), lax.rem(part + PARTS - 1, PARTS)
    for ref, place in ((mine_ref, part), (low_ref, below), (high_ref, above)):
        rows_ref[:, pl.ds(pl.multiple_of(place * width, LANES), width)] = ref[...].reshape(
            slots, width
        )
    nt = (((1,), (1,)), ((), ()))
    upward = lax.dot_general(
        rows_ref[:, :model], w_down_ref[...], nt, preferred_element_type=F32
    )
    weight = rows_ref[:, model : model + LANES].astype(F32)[:, :1]
    gate_pre, up_pre = gate_ref[...], up_ref[...]
    sigmoid = jax.nn.sigmoid(gate_pre)
    activated = gate_pre * sigmoid
    hidden = activated * up_pre
    part_prob = jnp.sum(hidden * upward, axis=1, keepdims=True)
    hidden_grad = weight * upward
    gate_grad = (hidden_grad * up_pre * sigmoid * (1.0 + gate_pre * (1.0 - sigmoid))).astype(BF16)
    up_grad = (hidden_grad * activated).astype(BF16)
    gate_grad_ref[...] = gate_grad
    up_grad_ref[...] = up_grad
    hidden_ref[...] = (hidden * weight).astype(BF16)
    grads = jnp.dot(gate_grad, w_gate_ref[...], preferred_element_type=F32)
    grads = grads + jnp.dot(up_grad, w_up_ref[...], preferred_element_type=F32)
    stage_ref[:, :model] = grads.astype(BF16)
    stage_ref[:, model:] = jnp.broadcast_to(
        part_prob, (slots, PARTS * width - model)
    ).astype(BF16)
    for ref, place in ((own_ref, part), (to_high_ref, above), (to_low_ref, below)):
        ref[...] = stage_ref[:, pl.ds(pl.multiple_of(place * width, LANES), width)]


def sum_kernel(own_ref, low_ref, high_ref, out_ref):
    total = own_ref[...].astype(F32) + low_ref[...].astype(F32) + high_ref[...].astype(F32)
    out_ref[...] = total.reshape(out_ref.shape).astype(BF16)


def combine_kernel(cap, part_ref, back_ref, ids_ref, got_ref, out_ref):
    peers, own, width = out_ref.shape
    tokens = peers * own
    experts, _, _ = got_ref.shape
    slots = experts * cap
    got = got_ref[...].astype(F32).reshape(slots, width)
    back = back_ref[...]
    sums = jnp.dot(back, got.astype(BF16), preferred_element_type=F32)[:tokens]
    prob = got[:, width - LANES :].T[:1, :]
    picked = back[:tokens].astype(F32) * prob
    expert = lax.broadcasted_iota(jnp.int32, (tokens, slots), 1) // cap
    ids = ids_ref[...]
    lane = lax.broadcasted_iota(jnp.int32, (tokens, LANES), 1)
    by_choice = jnp.zeros((tokens, LANES), F32)
    for k in range(ids.shape[1]):
        one = jnp.sum(
            jnp.where(expert == ids[:, k : k + 1], picked, 0.0), axis=1, keepdims=True
        )
        by_choice = jnp.where(lane == k, one, by_choice)
    last = jnp.where(part_ref[0] == PARTS - 1, by_choice, sums[:, width - LANES :])
    sums = jnp.concatenate([sums[:, : width - LANES], last], axis=1)
    out_ref[...] = sums.reshape(peers, own, width)


def finish_kernel(got_ref, tokens_ref, probs_ref):
    peers, _, width = got_ref.shape
    model = tokens_ref.shape[1]
    for part in range(PARTS):
        total = got_ref[part]
        for peer in range(part + PARTS, peers, PARTS):
            total = total + got_ref[peer]
        low = part * width
        high = min(low + width, model)
        tokens_ref[:, low:high] = total[:, : high - low].astype(BF16)
        if part == PARTS - 1:
            probs_ref[...] = total[:, width - LANES : width - LANES + probs_ref.shape[1]]


def body(grad_out, probs, expert_ids, saved_inputs, w_gate, w_up, w_down):
    tp_count = lax.axis_size("tp")
    experts, cap, model = saved_inputs.shape[1:]
    slots = experts * cap
    own, top = grad_out.shape[1], expert_ids.shape[2]
    tokens = tp_count * own
    width = -(-(model + LANES) // (PARTS * LANES)) * LANES
    units = w_down.shape[1]
    wide = tokens + 8
    part = lax.rem(lax.axis_index("tp"), PARTS).astype(jnp.int32).reshape(1)
    rise = [(i, (i + 1) % tp_count) for i in range(tp_count)]
    fall = [(i, (i - 1) % tp_count) for i in range(tp_count)]

    padded = jnp.pad(grad_out[0], ((0, 0), (0, PARTS * width - model)))
    thirds = padded.reshape(own, PARTS, width).transpose(1, 0, 2)
    column = lax.all_to_all(
        jnp.tile(thirds, (tp_count // PARTS, 1, 1)), "tp", split_axis=0, concat_axis=0, tiled=True
    )
    ids = expert_ids[0]
    pick, back = call(
        lambda *refs: route_kernel(cap, *refs),
        [
            jax.ShapeDtypeStruct((slots, wide), BF16),
            jax.ShapeDtypeStruct((wide, slots), BF16),
        ],
        [VMEM] * 2,
        1000000,
        100000,
    )(ids.T, probs[0].T)
    sent = call(
        send_kernel,
        jax.ShapeDtypeStruct((experts, cap, width), BF16),
        [SMEM, VMEM, VMEM],
        2 * slots * wide * width,
        2 * slots * width,
    )(part, pick, column)
    mine = lax.all_to_all(sent, COLUMN, split_axis=0, concat_axis=0, tiled=True)
    low = lax.ppermute(mine, "tp", rise)
    high = lax.ppermute(mine, "tp", fall)

    rows_input = saved_inputs[0].reshape(slots, model)
    gate_pre = jnp.dot(rows_input, w_gate[0], preferred_element_type=F32)
    up_pre = jnp.dot(rows_input, w_up[0], preferred_element_type=F32)
    slab = jax.ShapeDtypeStruct((slots, width), BF16)
    thin = jax.ShapeDtypeStruct((slots, units), BF16)
    mine_grad, to_high, to_low, rows, gate_grad, up_grad, hidden = call(
        expert_kernel,
        [slab, slab, slab, jax.ShapeDtypeStruct((slots, PARTS * width), BF16), thin, thin, thin],
        [SMEM] + [VMEM] * 8,
        6 * slots * model * units,
        12 * slots * model,
        (pltpu.VMEM((slots, PARTS * width), BF16),),
    )(part, mine, low, high, gate_pre, up_pre, w_gate[0].T, w_up[0].T, w_down[0])
    from_low = lax.ppermute(to_high, "tp", rise)
    from_high = lax.ppermute(to_low, "tp", fall)

    tn = (((0,), (0,)), ((), ()))
    grad_gate = lax.dot_general(rows_input, gate_grad, tn, preferred_element_type=F32)
    grad_up = lax.dot_general(rows_input, up_grad, tn, preferred_element_type=F32)
    grad_down = lax.dot_general(hidden, rows[:, :model], tn, preferred_element_type=F32)

    summed = call(
        sum_kernel,
        jax.ShapeDtypeStruct((experts, cap, width), BF16),
        [VMEM] * 3,
        3 * slots * width,
        8 * slots * width,
    )(mine_grad, from_low, from_high)
    got = lax.all_to_all(summed, COLUMN, split_axis=0, concat_axis=0, tiled=True)
    combined = call(
        lambda *refs: combine_kernel(cap, *refs),
        jax.ShapeDtypeStruct((tp_count, own, width), F32),
        [SMEM] + [VMEM] * 3,
        2 * slots * wide * width,
        2 * slots * width,
    )(part, back, ids, got)
    last = lax.all_to_all(combined, "tp", split_axis=0, concat_axis=0, tiled=True)
    grad_tokens, grad_probs = call(
        finish_kernel,
        [
            jax.ShapeDtypeStruct((own, model), BF16),
            jax.ShapeDtypeStruct((own, top), F32),
        ],
        [VMEM],
        1000,
        4 * tokens * width,
    )(last)
    return (
        grad_tokens[None],
        grad_probs[None],
        grad_gate.astype(BF16)[None],
        grad_up.astype(BF16)[None],
        grad_down.astype(BF16)[None],
    )


def solution(mesh):
    placed = (
        P(COLUMN, "tp", None),
        P(COLUMN, None, None),
        P(COLUMN, None, None),
        P(COLUMN, None, None, None),
        P(COLUMN, None, "tp"),
        P(COLUMN, None, "tp"),
        P(COLUMN, "tp", None),
    )
    return jax.shard_map(
        body,
        mesh=mesh,
        in_specs=placed,
        out_specs=(
            P(COLUMN, "tp", None),
            P(COLUMN, "tp", None),
            P(COLUMN, None, "tp"),
            P(COLUMN, None, "tp"),
            P(COLUMN, "tp", None),
        ),
        check_vma=False,
    )
```

time: 246 us -> 161 us (0.65)
  blocking collectives: 76.3 us -> 32.2 us
  waiting for transfers between devices: 92.9 us -> 55.2 us
  local copies, waits for them, and re-layouts: 22.6 us -> 11.5 us
  Pallas kernels: 0 us -> 7.31 us
  starting transfers between devices: 38.5 us -> 41.4 us
    all_to_all x4 -> x3, waiting for transfers between devices: 92.9 us -> 36 us  [the longest x1 18.8 us: body(): lax.all_to_all(summed, COLUMN, split_axis=0, concat_axis=0, tiled=True)]
    unnamed x1 -> x0, blocking collectives: 44.7 us -> none
    all_to_all x0 -> x1, blocking collectives: none -> 32.2 us  [body(): mine = lax.all_to_all(sent, COLUMN, split_axis=0, concat_axis=0, tiled=True)]
    all_gather x1 -> x0, blocking collectives: 31.6 us -> none  [body(): column = lax.all_gather(grad_out, 'tp', axis=1, tiled=True)[0]]
    ppermute x0 -> x4, waiting for transfers between devices: none -> 19.2 us  [the longest x1 12.7 us: body(): from_low = lax.ppermute(to_high, 'tp', rise)]
    ppermute x0 -> x4, starting transfers between devices: none -> 14.7 us  [the longest x1 5.52 us: body(): from_high = lax.ppermute(to_low, 'tp', fall)]
    reshape x5 -> x1, local copies, waits for them, and re-layouts: 13 us -> 0.04 us  [body(): thirds = padded.reshape(own, PARTS, width).transpose(1, 0, 2)]
    all_to_all x4 -> x3, starting transfers between devices: 38.5 us -> 26.7 us  [the longest x1 15.2 us: body(): lax.all_to_all(jnp.tile(thirds, (tp_count // PARTS, 1, 1)), 'tp', split_a...]
  transfers between devices with their start and end apart: 4 -> 7, of which waited for: 3 -> 7; matrix products, arithmetic and copies ran while one was open for 9% -> 10% of each run, Pallas kernels for 0% -> 0%
where the time goes in v1:
time: 161 us; the launch traced here: 160 us
  waiting for transfers between devices  55.2 us (34%)
  starting transfers between devices  41.4 us (26%)
  blocking collectives  32.2 us (20%)
  matrix products  11.7 us (7%)
  local copies, waits for them, and re-layouts  11.5 us (7%)
  Pallas kernels  7.31 us (5%)
    all_to_all x1, blocking collectives, body(): mine = lax.all_to_all(sent, COLUMN, split_axis=0, concat_axis=0, tiled=True)  32.2 us
    all_to_all x1, waiting for transfers between devices, body(): lax.all_to_all(summed, COLUMN, split_axis=0, concat_axis=0, tiled=True)  18.8 us
    all_to_all x1, starting transfers between devices, body(): lax.all_to_all(jnp.tile(thirds, (tp_count // PARTS, 1, 1)), 'tp', split_a...  15.2 us
    ppermute x1, waiting for transfers between devices, body(): from_low = lax.ppermute(to_high, 'tp', rise)  12.7 us
    all_to_all x1, waiting for transfers between devices, body(): lax.all_to_all(jnp.tile(thirds, (tp_count // PARTS, 1, 1)), 'tp', split_a...  9.34 us
    all_to_all x1, waiting for transfers between devices, body(): lax.all_to_all(combined, 'tp', split_axis=0, concat_axis=0, tiled=True)  7.88 us
    all_to_all x1, starting transfers between devices, body(): lax.all_to_all(summed, COLUMN, split_axis=0, concat_axis=0, tiled=True)  6.57 us
    unnamed x25, local copies, waits for them, and re-layouts  6.02 us
  transfers between devices with their start and end apart: 7, of which 7 were waited for; matrix products, arithmetic and copies ran while one was open for 10% of the time, Pallas kernels for 0%

profile of v1, /device:TPU:2, one launch (start us, length us, event | category | flops | bytes accessed | tf_op | source)
XLA Modules:
  0.0 160.2 jit_solution(6881244088008360031)
XLA Ops:
  0.6 0.7 pad.4
  1.4 0.7 tile.4
  2.1 15.2 %all-to-all-start = ((bf16[12,2,1408]{2,1,0:T(2,128)(2,1)}), bf16[12,2,1408]{2,1,0:T(2,128)(2,1)S(1)}, u32[]{:S(2)}, u32[]{:S(2)}) async-start(bf16[12,2,1408]{2,1,0:T(2,128)(2,1)} %bitcast.8), calls=%async_computation | async-start | bytes 135168 | tf_op jit(solution)/shard_map/all_to_all | solution.py:169
  17.3 0.0 copy-start.9
  17.3 0.7 copy-done.9
  18.0 0.0 copy-start.11
  18.0 0.7 copy-done.11
  18.7 0.4 shard_map.110
  19.1 9.3 %all-to-all-done.column_ref = bf16[12,2,1408]{2,1,0:T(2,128)(2,1)S(1)} async-done(((bf16[12,2,1408]{2,1,0:T(2,128)(2,1)}), bf16[12,2,1408]{2,1,0:T(2,128)(2,1)S(1)}, u32[]{:S(2)}, u32[]{:S(2)}) %all-to-all-start) | async-done | bytes 67616 | tf_op jit(solution)/shard_map/all_to_all | solution.py:169
  28.4 0.4 shard_map.111
  28.8 32.2 %all_to_all.20.mine_ref = bf16[64,4,1408]{2,1,0:T(4,128)(2,1)S(1)} all-to-all(bf16[64,4,1408]{2,1,0:T(4,128)(2,1)S(1)} %shard_map.111), channel_id=1, replica_groups=mesh['dp'=8,'ctx'=8,'tp'=12] {'dp','ctx'}, dimensions={0} | all-to-all | bytes 1441792 | tf_op jit(solution)/shard_map/all_to_all | solution.py:190
  61.0 0.0 copy-start.1
  61.0 2.6 %collective-permute-start = (bf16[64,4,1408]{2,1,0:T(4,128)(2,1)S(1)}, bf16[64,4,1408]{2,1,0:T(4,128)(2,1)S(1)}, u32[]{:S(2)}, u32[]{:S(2)}) collective-permute-start(bf16[64,4,1408]{2,1,0:T(4,128)(2,1)S(1)} %all_to_all.20.mine_ref), channel_id=1, source_target_pairs={{0,1},{1,2},{2,3},{3,4},{4,5},{5,6},{6,7},{7,8},{8,9},{9,10},{10,1... | collective-permute-start | bytes 2162696 | tf_op jit(solution)/shard_map/ppermute | solution.py:191
  63.6 4.6 %collective-permute-start.1 = (bf16[64,4,1408]{2,1,0:T(4,128)(2,1)S(1)}, bf16[64,4,1408]{2,1,0:T(4,128)(2,1)S(1)}, u32[]{:S(2)}, u32[]{:S(2)}) collective-permute-start(bf16[64,4,1408]{2,1,0:T(4,128)(2,1)S(1)} %all_to_all.20.mine_ref), channel_id=1, source_target_pairs={{0,11},{1,0},{2,1},{3,2},{4,3},{5,4},{6,5},{7,6},{8,7},{9,8},{10,9... | collective-permute-start | bytes 2162696 | tf_op jit(solution)/shard_map/ppermute | solution.py:192
  68.2 4.0 %reshape_squeeze.3 = bf16[256,4096]{1,0:T(8,128)(2,1)} reshape(bf16[1,64,4,4096]{3,2,1,0:T(4,128)(2,1)} %param.10) | data formatting | bytes 4194304 | tf_op jit(solution)/shard_map/reshape;squeeze | solution.py:194
  72.2 0.0 copy-done.1
  72.2 0.0 copy-start
  72.2 0.0 copy-start.6
  72.2 2.4 %fusion.4.up_ref = f32[256,64]{1,0:T(8,128)S(1)} fusion(bf16[256,4096]{1,0:T(8,128)(2,1)} %reshape_squeeze.3, bf16[1,4096,64]{1,2,0:T(8,128)(2,1)S(1)} %copy-done.1), kind=kOutput, calls=%fused_computation.7 | convolution fusion | flops 134217728 | bytes 2686976 | tf_op jit(solution)/shard_map/dot_general | solution.py:196
  74.6 0.0 copy-done
  74.6 2.3 %fusion.6.gate_ref = f32[256,64]{1,0:T(8,128)S(1)} fusion(bf16[256,4096]{1,0:T(8,128)(2,1)} %reshape_squeeze.3, bf16[1,4096,64]{1,2,0:T(8,128)(2,1)S(1)} %copy-done), kind=kOutput, calls=%fused_computation.9 | convolution fusion | flops 134217728 | bytes 2686976 | tf_op jit(solution)/shard_map/dot_general | solution.py:195
  76.9 5.0 %collective-permute-done.low_ref = bf16[64,4,1408]{2,1,0:T(4,128)(2,1)S(1)} collective-permute-done((bf16[64,4,1408]{2,1,0:T(4,128)(2,1)S(1)}, bf16[64,4,1408]{2,1,0:T(4,128)(2,1)S(1)}, u32[]{:S(2)}, u32[]{:S(2)}) %collective-permute-start) | collective-permute-done | bytes 720928 | tf_op jit(solution)/shard_map/ppermute | solution.py:191
  81.8 0.0 copy-start.2
  81.8 0.9 copy-done.2
  82.7 0.3 collective-permute-done.1.high_ref
  83.0 0.0 copy-start.4
  83.0 0.9 copy-done.4
  83.9 0.0 copy-done.6
  83.9 0.0 copy-start.3
  83.9 1.1 copy-done.3
  85.0 0.0 copy-start.5
  85.0 1.1 copy-done.5
  86.1 3.4 %shard_map.112 = (bf16[256,1408]{1,0:T(8,128)(2,1)S(1)}, bf16[256,1408]{1,0:T(8,128)(2,1)S(1)}, bf16[256,1408]{1,0:T(8,128)(2,1)S(1)}, bf16[256,4224]{1,0:T(8,12...) custom-call(s32[1]{0:T(128)} %bitcast.part_ref.refs_0_, ...), custom_call_target="tpu_custom_call" | custom-call | flops 402653184 | bytes 12582912 | tf_op jit(solution)/shard_map/pallas_call | solution.py:199
  89.5 0.0 copy-start.7
  89.5 0.6 copy-done.7
  90.1 2.0 %collective-permute-start.2 = (bf16[256,1408]{1,0:T(8,128)(2,1)S(1)}, bf16[256,1408]{1,0:T(8,128)(2,1)S(1)}, u32[]{:S(2)}, u32[]{:S(2)}) collective-permute-start(bf16[256,1408]{1,0:T(8,128)(2,1)S(1)} %get-tuple-element.19), channel_id=1, source_target_pairs={{0,1},{1,2},{2,3},{3,4},{4,5},{5,6},{6,7},{7,8},{8,9},{9,10},{10,1... | collective-permute-start | bytes 2162696 | tf_op jit(solution)/shard_map/ppermute | solution.py:207
  92.1 5.5 %collective-permute-start.3 = (bf16[256,1408]{1,0:T(8,128)(2,1)S(1)}, bf16[256,1408]{1,0:T(8,128)(2,1)S(1)}, u32[]{:S(2)}, u32[]{:S(2)}) collective-permute-start(bf16[256,1408]{1,0:T(8,128)(2,1)S(1)} %get-tuple-element.20), channel_id=1, source_target_pairs={{0,11},{1,0},{2,1},{3,2},{4,3},{5,4},{6,5},{7,6},{8,7},{9,8},{10,9... | collective-permute-start | bytes 2162696 | tf_op jit(solution)/shard_map/ppermute | solution.py:208
  97.6 12.7 %collective-permute-done.2.low_ref = bf16[256,1408]{1,0:T(8,128)(2,1)S(1)} collective-permute-done((bf16[256,1408]{1,0:T(8,128)(2,1)S(1)}, bf16[256,1408]{1,0:T(8,128)(2,1)S(1)}, u32[]{:S(2)}, u32[]{:S(2)}) %collective-permute-start.2) | collective-permute-done | bytes 720928 | tf_op jit(solution)/shard_map/ppermute | solution.py:207
  110.4 1.2 collective-permute-done.3.high_ref
  111.6 0.0 copy-start.10
  111.6 0.0 copy-start.8
  111.6 1.3 shard_map.113
  112.9 6.6 %all-to-all-start.2 = ((bf16[64,4,1408]{2,1,0:T(4,128)(2,1)}), bf16[64,4,1408]{2,1,0:T(4,128)(2,1)S(1)}, u32[]{:S(2)}, u32[]{:S(2)}) async-start(bf16[64,4,1408]{2,1,0:T(4,128)(2,1)} %shard_map.113), calls=%async_computation.2 | async-start | bytes 1441792 | tf_op jit(solution)/shard_map/all_to_all | solution.py:222
  119.5 0.0 copy-done.10
  119.5 0.1 copy.17
  119.5 0.0 copy-done.8
  119.5 2.9 %fusion = bf16[1,4096,64]{1,2,0:T(8,128)(2,1)} fusion(bf16[256,64]{1,0:T(8,128)(2,1)S(1)} %copy-done.8, bf16[256,4096]{1,0:T(8,128)(2,1)} %reshape_squeeze.3), kind=kOutput, calls=%fused_computation.3 | convolution fusion | flops 134479872 | bytes 2654208 | tf_op jit(solution)/shard_map/dot_general | solution.py:211
  122.4 18.8 %all-to-all-done.2.refs_3_ = bf16[64,4,1408]{2,1,0:T(4,128)(2,1)S(1)} async-done(((bf16[64,4,1408]{2,1,0:T(4,128)(2,1)}), bf16[64,4,1408]{2,1,0:T(4,128)(2,1)S(1)}, u32[]{:S(2)}, u32[]{:S(2)}) %all-to-all-start.2) | async-done | bytes 720928 | tf_op jit(solution)/shard_map/all_to_all | solution.py:222
  141.2 1.2 shard_map.114
  142.4 5.0 %all-to-all-start.3 = ((f32[12,2,1408]{2,1,0:T(2,128)}), f32[12,2,1408]{2,1,0:T(2,128)S(1)}, u32[]{:S(2)}, u32[]{:S(2)}) async-start(f32[12,2,1408]{2,1,0:T(2,128)} %shard_map.114), calls=%async_computation.3 | async-start | bytes 270336 | tf_op jit(solution)/shard_map/all_to_all | solution.py:230
  147.5 2.9 %fusion.1 = bf16[1,4096,64]{1,2,0:T(8,128)(2,1)} fusion(bf16[256,64]{1,0:T(8,128)(2,1)S(1)} %get-tuple-element.24, bf16[256,4096]{1,0:T(8,128)(2,1)} %reshape_squeeze.3), kind=kOutput, calls=%fused_computation.4 | convolution fusion | flops 134479872 | bytes 2654208 | tf_op jit(solution)/shard_map/dot_general | solution.py:212
  150.3 1.3 fusion.2
  151.6 7.9 %all-to-all-done.3.got_ref = f32[12,2,1408]{2,1,0:T(2,128)S(1)} async-done(((f32[12,2,1408]{2,1,0:T(2,128)}), f32[12,2,1408]{2,1,0:T(2,128)S(1)}, u32[]{:S(2)}, u32[]{:S(2)}) %all-to-all-start.3) | async-done | bytes 135200 | tf_op jit(solution)/shard_map/all_to_all | solution.py:230
  159.5 0.6 shard_map.115
  (2 shorter events, 0.1 us)
Async XLA Ops:
  2.1 26.3 %all-to-all-start = ((bf16[12,2,1408]{2,1,0:T(2,128)(2,1)}), bf16[12,2,1408]{2,1,0:T(2,128)(2,1)S(1)}, u32[]{:S(2)}, u32[]{:S(2)}) async-start(bf16[12,2,1408]{2,1,0:T(2,128)(2,1)} %bitcast.8), calls=%async_computation | async-start | bytes 135168 | tf_op jit(solution)/shard_map/all_to_all | solution.py:169
  17.3 0.7 copy-start.9
  18.0 0.7 copy-start.11
  61.0 11.2 %copy-start.1 = (bf16[1,4096,64]{1,2,0:T(8,128)(2,1)S(1)}, bf16[1,4096,64]{1,2,0:T(8,128)(2,1)}, u32[]{:S(2)}) copy-start(bf16[1,4096,64]{1,2,0:T(8,128)(2,1)} %param.12) | copy-start | bytes 1572868
  61.0 20.8 %collective-permute-start = (bf16[64,4,1408]{2,1,0:T(4,128)(2,1)S(1)}, bf16[64,4,1408]{2,1,0:T(4,128)(2,1)S(1)}, u32[]{:S(2)}, u32[]{:S(2)}) collective-permute-start(bf16[64,4,1408]{2,1,0:T(4,128)(2,1)S(1)} %all_to_all.20.mine_ref), channel_id=1, source_target_pairs={{0,1},{1,2},{2,3},{3,4},{4,5},{5,6},{6,7},{7,8},{8,9},{9,10},{10,1... | collective-permute-start | bytes 2162696 | tf_op jit(solution)/shard_map/ppermute | solution.py:191
  63.6 19.4 %collective-permute-start.1 = (bf16[64,4,1408]{2,1,0:T(4,128)(2,1)S(1)}, bf16[64,4,1408]{2,1,0:T(4,128)(2,1)S(1)}, u32[]{:S(2)}, u32[]{:S(2)}) collective-permute-start(bf16[64,4,1408]{2,1,0:T(4,128)(2,1)S(1)} %all_to_all.20.mine_ref), channel_id=1, source_target_pairs={{0,11},{1,0},{2,1},{3,2},{4,3},{5,4},{6,5},{7,6},{8,7},{9,8},{10,9... | collective-permute-start | bytes 2162696 | tf_op jit(solution)/shard_map/ppermute | solution.py:192
  72.2 2.4 %copy-start = (bf16[1,4096,64]{1,2,0:T(8,128)(2,1)S(1)}, bf16[1,4096,64]{1,2,0:T(8,128)(2,1)}, u32[]{:S(2)}) copy-start(bf16[1,4096,64]{1,2,0:T(8,128)(2,1)} %param.11) | copy-start | bytes 1572868
  72.2 11.7 %copy-start.6 = (bf16[1,64,4096]{2,1,0:T(8,128)(2,1)S(1)}, bf16[1,64,4096]{2,1,0:T(8,128)(2,1)}, u32[]{:S(2)}) copy-start(bf16[1,64,4096]{2,1,0:T(8,128)(2,1)} %param.13) | copy-start | bytes 1572868
  81.8 0.9 copy-start.2
  83.0 0.9 copy-start.4
  83.9 1.1 copy-start.3
  85.0 1.1 copy-start.5
  89.5 0.6 copy-start.7
  90.1 20.3 %collective-permute-start.2 = (bf16[256,1408]{1,0:T(8,128)(2,1)S(1)}, bf16[256,1408]{1,0:T(8,128)(2,1)S(1)}, u32[]{:S(2)}, u32[]{:S(2)}) collective-permute-start(bf16[256,1408]{1,0:T(8,128)(2,1)S(1)} %get-tuple-element.19), channel_id=1, source_target_pairs={{0,1},{1,2},{2,3},{3,4},{4,5},{5,6},{6,7},{7,8},{8,9},{9,10},{10,1... | collective-permute-start | bytes 2162696 | tf_op jit(solution)/shard_map/ppermute | solution.py:207
  92.1 19.4 %collective-permute-start.3 = (bf16[256,1408]{1,0:T(8,128)(2,1)S(1)}, bf16[256,1408]{1,0:T(8,128)(2,1)S(1)}, u32[]{:S(2)}, u32[]{:S(2)}) collective-permute-start(bf16[256,1408]{1,0:T(8,128)(2,1)S(1)} %get-tuple-element.20), channel_id=1, source_target_pairs={{0,11},{1,0},{2,1},{3,2},{4,3},{5,4},{6,5},{7,6},{8,7},{9,8},{10,9... | collective-permute-start | bytes 2162696 | tf_op jit(solution)/shard_map/ppermute | solution.py:208
  111.6 7.9 %copy-start.10 = (s32[1,24,8]{1,2,0:T(8,128)S(1)}, s32[1,24,8]{1,2,0:T(8,128)}, u32[]{:S(2)}) copy-start(s32[1,24,8]{1,2,0:T(8,128)} %param.9) | copy-start | bytes 2308
  111.6 8.0 %copy-start.8 = (bf16[256,64]{1,0:T(8,128)(2,1)S(1)}, bf16[256,64]{1,0:T(8,128)(2,1)}, u32[]{:S(2)}) copy-start(bf16[256,64]{1,0:T(8,128)(2,1)} %copy-done.7) | copy-start | bytes 98308
  112.9 28.4 %all-to-all-start.2 = ((bf16[64,4,1408]{2,1,0:T(4,128)(2,1)}), bf16[64,4,1408]{2,1,0:T(4,128)(2,1)S(1)}, u32[]{:S(2)}, u32[]{:S(2)}) async-start(bf16[64,4,1408]{2,1,0:T(4,128)(2,1)} %shard_map.113), calls=%async_computation.2 | async-start | bytes 1441792 | tf_op jit(solution)/shard_map/all_to_all | solution.py:222
  142.4 17.1 %all-to-all-start.3 = ((f32[12,2,1408]{2,1,0:T(2,128)}), f32[12,2,1408]{2,1,0:T(2,128)S(1)}, u32[]{:S(2)}, u32[]{:S(2)}) async-start(f32[12,2,1408]{2,1,0:T(2,128)} %shard_map.114), calls=%async_computation.3 | async-start | bytes 270336 | tf_op jit(solution)/shard_map/all_to_all | solution.py:230

commit v2 on v1

v2 whole, which is shorter than its diff:
```python
import jax
import jax.numpy as jnp
from jax import lax
from jax.experimental import pallas as pl
from jax.experimental.pallas import tpu as pltpu
from jax.sharding import PartitionSpec as P

PARTS = 3
LANES = 128
F32, BF16 = jnp.float32, jnp.bfloat16
COLUMN = ("dp", "ctx")
VMEM = pl.BlockSpec(memory_space=pltpu.VMEM)
SMEM = pl.BlockSpec(memory_space=pltpu.SMEM)


def call(kernel, outs, in_specs, flops, bytes_accessed, scratch=()):
    return pl.pallas_call(
        kernel,
        out_shape=outs,
        in_specs=in_specs,
        out_specs=jax.tree.map(lambda _: VMEM, outs),
        scratch_shapes=scratch,
        compiler_params=pltpu.CompilerParams(vmem_limit_bytes=16 << 20),
        cost_estimate=pl.CostEstimate(
            flops=flops, bytes_accessed=bytes_accessed, transcendentals=0
        ),
    )


def route_kernel(cap, ids_ref, probs_ref, pick_ref, back_ref):
    top, tokens = ids_ref.shape
    slots, width = pick_ref.shape
    row = lax.broadcasted_iota(jnp.int32, (slots, tokens), 0)
    expert, place = row // cap, row % cap
    ids = ids_ref[...]
    probs = probs_ref[...].astype(F32)
    member = jnp.zeros((slots, tokens), F32)
    weight = jnp.zeros((slots, tokens), F32)
    for k in range(top):
        same = expert == ids[k : k + 1, :]
        member = jnp.where(same, 1.0, member)
        weight = jnp.where(same, probs[k : k + 1, :], weight)
    before = lax.broadcasted_iota(jnp.int32, (tokens, tokens), 0) < lax.broadcasted_iota(
        jnp.int32, (tokens, tokens), 1
    )
    rank = jnp.dot(
        member.astype(BF16), before.astype(F32).astype(BF16), preferred_element_type=F32
    )
    pick = jnp.where(rank == place.astype(F32), member, 0.0)
    slot_weight = jnp.sum(pick * weight, axis=1, keepdims=True)
    tail = lax.broadcasted_iota(jnp.int32, (slots, width - tokens), 1)
    full = jnp.concatenate([pick, jnp.where(tail == 0, slot_weight, 0.0)], axis=1)
    pick_ref[...] = full.astype(BF16)
    back_ref[...] = full.T.astype(BF16)


def thirds_kernel(grad_ref, out_ref):
    peers, _, width = out_ref.shape
    model = grad_ref.shape[1]
    for part in range(PARTS):
        piece = grad_ref[:, part * width : min(part * width + width, model)]
        if piece.shape[1] < width:
            piece = jnp.concatenate(
                [piece, jnp.zeros((piece.shape[0], width - piece.shape[1]), BF16)], axis=1
            )
        for peer in range(part, peers, PARTS):
            out_ref[peer] = piece


def weights_kernel(part_ref, gate_ref, up_ref, down_ref, own_ref, high_ref, low_ref, stage_ref):
    units, model = gate_ref.shape
    width = own_ref.shape[1]
    part = part_ref[0]
    above, below = lax.rem(part + 1, PARTS), lax.rem(part + PARTS - 1, PARTS)
    for at, ref in enumerate((gate_ref, up_ref, down_ref)):
        stage_ref[at * units : (at + 1) * units, :model] = ref[...]
    stage_ref[:, model:] = jnp.zeros((PARTS * units, PARTS * width - model), BF16)
    for ref, place in ((own_ref, part), (high_ref, above), (low_ref, below)):
        ref[...] = stage_ref[:, pl.ds(pl.multiple_of(place * width, LANES), width)]


def send_kernel(part_ref, pick_ref, column_ref, out_ref):
    peers, own, width = column_ref.shape
    tokens = peers * own
    experts, cap, _ = out_ref.shape
    column = column_ref[...].astype(F32).reshape(tokens, width)
    rest = pick_ref.shape[1] - tokens
    lane = lax.broadcasted_iota(jnp.int32, (rest, width), 1)
    deep = lax.broadcasted_iota(jnp.int32, (rest, width), 0)
    padded = (deep == 0) & (lane >= width - LANES) & (part_ref[0] == PARTS - 1)
    column = jnp.concatenate([column, padded.astype(F32)], axis=0).astype(BF16)
    rows = jnp.dot(pick_ref[...], column, preferred_element_type=F32)
    out_ref[...] = rows.reshape(experts, cap, width).astype(BF16)


def upward_kernel(part_ref, got_ref, own_w_ref, low_w_ref, high_w_ref, rows_ref, own_ref, to_low_ref, to_high_ref):
    experts, cap, width = got_ref.shape
    slots, units = experts * cap, own_w_ref.shape[0] // 3
    rows = got_ref[...].reshape(slots, width)
    rows_ref[...] = rows
    nt = (((1,), (1,)), ((), ()))
    weight = jnp.where(
        part_ref[0] == PARTS - 1, rows[:, width - LANES : width - LANES + units].astype(F32), 0.0
    )
    for w_ref, ref in ((own_w_ref, own_ref), (low_w_ref, to_low_ref), (high_w_ref, to_high_ref)):
        product = lax.dot_general(rows, w_ref[2 * units :], nt, preferred_element_type=F32)
        ref[...] = jnp.concatenate([product, weight], axis=1)


def expert_kernel(own_ref, low_ref, high_ref, gate_ref, up_ref, out_ref):
    slots, units = gate_ref.shape
    total = own_ref[...] + low_ref[...] + high_ref[...]
    upward, weight = total[:, :units], total[:, units:]
    gate_pre, up_pre = gate_ref[...], up_ref[...]
    sigmoid = jax.nn.sigmoid(gate_pre)
    activated = gate_pre * sigmoid
    hidden = activated * up_pre
    part_prob = jnp.sum(hidden * upward, axis=1, keepdims=True)
    hidden_grad = weight * upward
    gate_grad = hidden_grad * up_pre * sigmoid * (1.0 + gate_pre * (1.0 - sigmoid))
    up_grad = hidden_grad * activated
    lane = lax.broadcasted_iota(jnp.int32, (slots, units), 1)
    high = part_prob.astype(BF16).astype(F32)
    prob = jnp.where(lane == 0, high, part_prob - high)
    both = jnp.concatenate([gate_grad, up_grad], axis=1)
    rest = jnp.concatenate([hidden * weight, prob], axis=1)
    out_ref[...] = jnp.concatenate([both, rest], axis=1).astype(BF16)


def back_kernel(part_ref, own_ref, low_ref, high_ref, own_w_ref, low_w_ref, high_w_ref, out_ref):
    experts, cap, width = out_ref.shape
    slots, units = own_ref.shape[0], own_ref.shape[1] // 4
    pairs = ((own_ref, own_w_ref), (low_ref, low_w_ref), (high_ref, high_w_ref))
    left = jnp.concatenate([ref[:, : 2 * units] for ref, _ in pairs], axis=1)
    right = jnp.concatenate([ref[: 2 * units] for _, ref in pairs], axis=0)
    grads = jnp.dot(left, right, preferred_element_type=F32)
    prob = jnp.zeros((slots, 1), F32)
    for ref, _ in pairs:
        prob = prob + jnp.sum(
            ref[:, 2 * units :].astype(F32)[:, units : units + 2], axis=1, keepdims=True
        )
    high = prob.astype(BF16).astype(F32)
    lane = lax.broadcasted_iota(jnp.int32, (slots, LANES), 1)
    prob = jnp.where(lane == 0, high, prob - high)
    last = jnp.where(part_ref[0] == PARTS - 1, prob, grads[:, width - LANES :])
    grads = jnp.concatenate([grads[:, : width - LANES], last], axis=1)
    out_ref[...] = grads.reshape(experts, cap, width).astype(BF16)


def down_kernel(rows_ref, own_ref, low_ref, high_ref, own_out_ref, low_out_ref, high_out_ref):
    units = own_ref.shape[1] // 4
    tn = (((0,), (0,)), ((), ()))
    left = jnp.concatenate(
        [ref[:, 2 * units : 3 * units] for ref in (own_ref, low_ref, high_ref)], axis=1
    )
    grads = lax.dot_general(left, rows_ref[...], tn, preferred_element_type=F32).astype(BF16)
    for at, ref in enumerate((own_out_ref, low_out_ref, high_out_ref)):
        ref[...] = grads[at * units : (at + 1) * units]


def join_kernel(part_ref, own_ref, low_ref, high_ref, out_ref, stage_ref):
    units, width = own_ref.shape
    part = part_ref[0]
    above, below = lax.rem(part + 1, PARTS), lax.rem(part + PARTS - 1, PARTS)
    for ref, place in ((own_ref, part), (low_ref, below), (high_ref, above)):
        stage_ref[:, pl.ds(pl.multiple_of(place * width, LANES), width)] = ref[...]
    out_ref[...] = stage_ref[:, : out_ref.shape[1]]


def combine_kernel(cap, part_ref, back_ref, ids_ref, got_ref, out_ref):
    peers, own, width = out_ref.shape
    tokens = peers * own
    experts, _, _ = got_ref.shape
    slots = experts * cap
    got = got_ref[...].astype(F32).reshape(slots, width)
    back = back_ref[...]
    sums = jnp.dot(back, got.astype(BF16), preferred_element_type=F32)[:tokens]
    turned = got[:, width - LANES :].T
    prob = turned[:1, :] + turned[1:2, :]
    picked = back[:tokens].astype(F32) * prob
    expert = lax.broadcasted_iota(jnp.int32, (tokens, slots), 1) // cap
    ids = ids_ref[...]
    lane = lax.broadcasted_iota(jnp.int32, (tokens, LANES), 1)
    by_choice = jnp.zeros((tokens, LANES), F32)
    for k in range(ids.shape[1]):
        one = jnp.sum(
            jnp.where(expert == ids[:, k : k + 1], picked, 0.0), axis=1, keepdims=True
        )
        high = one.astype(BF16).astype(F32)
        by_choice = jnp.where(lane == k, high, by_choice)
        by_choice = jnp.where(lane == k + ids.shape[1], one - high, by_choice)
    last = jnp.where(part_ref[0] == PARTS - 1, by_choice, sums[:, width - LANES :])
    sums = jnp.concatenate([sums[:, : width - LANES], last], axis=1)
    out_ref[...] = sums.reshape(peers, own, width).astype(BF16)


def finish_kernel(got_ref, tokens_ref, probs_ref):
    peers, _, width = got_ref.shape
    model = tokens_ref.shape[1]
    for part in range(PARTS):
        total = got_ref[part].astype(F32)
        for peer in range(part + PARTS, peers, PARTS):
            total = total + got_ref[peer].astype(F32)
        low = part * width
        high = min(low + width, model)
        tokens_ref[:, low:high] = total[:, : high - low].astype(BF16)
        if part == PARTS - 1:
            top = probs_ref.shape[1]
            last = total[:, width - LANES :]
            probs_ref[...] = last[:, :top] + last[:, top : 2 * top]


def body(grad_out, probs, expert_ids, saved_inputs, w_gate, w_up, w_down):
    tp_count = lax.axis_size("tp")
    experts, cap, model = saved_inputs.shape[1:]
    slots = experts * cap
    own, top = grad_out.shape[1], expert_ids.shape[2]
    tokens = tp_count * own
    width = -(-(model + LANES) // (PARTS * LANES)) * LANES
    units = w_down.shape[1]
    wide = tokens + 8
    part = lax.rem(lax.axis_index("tp"), PARTS).astype(jnp.int32).reshape(1)

    def shape(*dims, dtype=BF16):
        return jax.ShapeDtypeStruct(dims, dtype)

    def trade(to_low, to_high):
        rise = [(i, (i + 1) % tp_count) for i in range(tp_count)]
        fall = [(i, (i - 1) % tp_count) for i in range(tp_count)]
        return lax.ppermute(to_high, "tp", rise), lax.ppermute(to_low, "tp", fall)

    thirds = call(thirds_kernel, shape(tp_count, own, width), [VMEM], 0, 100000)(grad_out[0])
    thirds, gate_rows, up_rows, down_rows = lax.optimization_barrier(
        (thirds, w_gate[0].T, w_up[0].T, w_down[0])
    )
    column = lax.all_to_all(thirds, "tp", split_axis=0, concat_axis=0, tiled=True)
    ids = expert_ids[0]
    pick, back = call(
        lambda *refs: route_kernel(cap, *refs),
        [shape(slots, wide), shape(wide, slots)],
        [VMEM] * 2,
        1000000,
        100000,
    )(ids.T, probs[0].T)
    slab = shape(3 * units, width)
    own_w, to_high_w, to_low_w = call(
        weights_kernel,
        [slab, slab, slab],
        [SMEM] + [VMEM] * 3,
        0,
        12 * units * model,
        (pltpu.VMEM((3 * units, PARTS * width), BF16),),
    )(part, gate_rows, up_rows, down_rows)
    low_w, high_w = trade(to_low_w, to_high_w)
    sent = call(
        send_kernel,
        shape(experts, cap, width),
        [SMEM, VMEM, VMEM],
        2 * slots * wide * width,
        2 * slots * width,
    )(part, pick, column)
    mine = lax.all_to_all(sent, COLUMN, split_axis=0, concat_axis=0, tiled=True)

    rows_input = saved_inputs[0].reshape(slots, model)
    gate_pre = jnp.dot(rows_input, w_gate[0], preferred_element_type=F32)
    up_pre = jnp.dot(rows_input, w_up[0], preferred_element_type=F32)
    mine, gate_pre, up_pre = lax.optimization_barrier((mine, gate_pre, up_pre))
    wide_sum = shape(slots, 2 * units, dtype=F32)
    rows, up_own, up_to_low, up_to_high = call(
        upward_kernel,
        [shape(slots, width), wide_sum, wide_sum, wide_sum],
        [SMEM] + [VMEM] * 4,
        6 * slots * width * units,
        4 * slots * width,
    )(part, mine, own_w, low_w, high_w)
    up_low, up_high = trade(up_to_low, up_to_high)
    terms = call(
        expert_kernel, shape(slots, 4 * units), [VMEM] * 5, 20 * slots * units, 20 * slots * units
    )(up_own, up_low, up_high, gate_pre, up_pre)
    low_terms, high_terms = trade(terms, terms)
    summed = call(
        back_kernel,
        shape(experts, cap, width),
        [SMEM] + [VMEM] * 6,
        12 * slots * width * units,
        2 * slots * width,
    )(part, terms, low_terms, high_terms, own_w, low_w, high_w)
    summed, terms, low_terms, high_terms = lax.optimization_barrier(
        (summed, terms, low_terms, high_terms)
    )
    got = lax.all_to_all(summed, COLUMN, split_axis=0, concat_axis=0, tiled=True)

    tn = (((0,), (0,)), ((), ()))
    strip = shape(units, width)
    down_own, down_to_low, down_to_high = call(
        down_kernel, [strip] * 3, [VMEM] * 4, 6 * slots * units * width, 2 * slots * width
    )(rows, terms, low_terms, high_terms)
    down_low, down_high = trade(down_to_low, down_to_high)
    grad_gate = lax.dot_general(
        rows_input, terms[:, :units], tn, preferred_element_type=F32
    )
    grad_up = lax.dot_general(
        rows_input, terms[:, units : 2 * units], tn, preferred_element_type=F32
    )
    grad_down = call(
        join_kernel,
        shape(units, model),
        [SMEM] + [VMEM] * 3,
        0,
        4 * units * model,
        (pltpu.VMEM((units, PARTS * width), BF16),),
    )(part, down_own, down_low, down_high)

    combined = call(
        lambda *refs: combine_kernel(cap, *refs),
        shape(tp_count, own, width),
        [SMEM] + [VMEM] * 3,
        2 * slots * wide * width,
        2 * slots * width,
    )(part, back, ids, got)
    last = lax.all_to_all(combined, "tp", split_axis=0, concat_axis=0, tiled=True)
    grad_tokens, grad_probs = call(
        finish_kernel,
        [shape(own, model), shape(own, top, dtype=F32)],
        [VMEM],
        1000,
        2 * tokens * width,
    )(last)
    return (
        grad_tokens[None],
        grad_probs[None],
        grad_gate.astype(BF16)[None],
        grad_up.astype(BF16)[None],
        grad_down[None],
    )


def solution(mesh):
    placed = (
        P(COLUMN, "tp", None),
        P(COLUMN, None, None),
        P(COLUMN, None, None),
        P(COLUMN, None, None, None),
        P(COLUMN, None, "tp"),
        P(COLUMN, None, "tp"),
        P(COLUMN, "tp", None),
    )
    return jax.shard_map(
        body,
        mesh=mesh,
        in_specs=placed,
        out_specs=(
            P(COLUMN, "tp", None),
            P(COLUMN, "tp", None),
            P(COLUMN, None, "tp"),
            P(COLUMN, None, "tp"),
            P(COLUMN, "tp", None),
        ),
        check_vma=False,
    )
```

time: 161 us -> 135 us (0.84)
  blocking collectives: 32.2 us -> 0 us
  starting transfers between devices: 41.4 us -> 69.8 us
  waiting for transfers between devices: 55.2 us -> 35.6 us
  local copies, waits for them, and re-layouts: 11.5 us -> 8.12 us
  Pallas kernels: 7.31 us -> 9.06 us
    all_to_all x1 -> x0, blocking collectives: 32.2 us -> none  [body(): mine = lax.all_to_all(sent, COLUMN, split_axis=0, concat_axis=0, tiled=True)]
    ppermute x4 -> x8, waiting for transfers between devices: 19.2 us -> 3.12 us  [trade(): return (lax.ppermute(to_high, 'tp', rise), lax.ppermute(to_low, 'tp', fall))]
    ppermute x4 -> x8, starting transfers between devices: 14.7 us -> 29.1 us  [trade(): return (lax.ppermute(to_high, 'tp', rise), lax.ppermute(to_low, 'tp', fall))]
    all_to_all x1 -> x2, starting transfers between devices: 15.2 us -> 25.8 us  [the longest x1 15.2 us: body(): lax.all_to_all(thirds, 'tp', split_axis=0, concat_axis=0, tiled=True)]
    all_to_all x1, waiting for transfers between devices: 18.8 us -> 10.8 us  [body(): lax.all_to_all(summed, COLUMN, split_axis=0, concat_axis=0, tiled=True)]
    all_to_all x1 -> x2, waiting for transfers between devices: 9.34 us -> 14.3 us  [the longest x1 9.34 us: body(): lax.all_to_all(thirds, 'tp', split_axis=0, concat_axis=0, tiled=True)]
    unnamed x25 -> x17, local copies, waits for them, and re-layouts: 6.02 us -> 2.28 us
    all_to_all x1, starting transfers between devices: 6.57 us -> 9.05 us  [body(): lax.all_to_all(summed, COLUMN, split_axis=0, concat_axis=0, tiled=True)]
  transfers between devices with their start and end apart: 7 -> 12, of which waited for: 7 -> 7; matrix products, arithmetic and copies ran while one was open for 10% -> 12% of each run, Pallas kernels for 0% -> 3%
where the time goes in v2:
time: 135 us; the launch traced here: 134 us
  starting transfers between devices  69.8 us (52%)
  waiting for transfers between devices  35.6 us (26%)
  matrix products  10.4 us (8%)
  Pallas kernels  9.06 us (7%)
  local copies, waits for them, and re-layouts  8.12 us (6%)
    ppermute x8, starting transfers between devices, trade(): return (lax.ppermute(to_high, 'tp', rise), lax.ppermute(to_low, 'tp', fall))  29.1 us
    all_to_all x1, starting transfers between devices, body(): lax.all_to_all(thirds, 'tp', split_axis=0, concat_axis=0, tiled=True)  15.2 us
    all_to_all x1, waiting for transfers between devices, body(): lax.all_to_all(summed, COLUMN, split_axis=0, concat_axis=0, tiled=True)  10.8 us
    all_to_all x1, starting transfers between devices, body(): mine = lax.all_to_all(sent, COLUMN, split_axis=0, concat_axis=0, tiled=True)  10.6 us
    all_to_all x1, waiting for transfers between devices, body(): lax.all_to_all(thirds, 'tp', split_axis=0, concat_axis=0, tiled=True)  9.34 us
    all_to_all x1, starting transfers between devices, body(): lax.all_to_all(summed, COLUMN, split_axis=0, concat_axis=0, tiled=True)  9.05 us
    all_to_all x1, waiting for transfers between devices, body(): lax.all_to_all(combined, 'tp', split_axis=0, concat_axis=0, tiled=True)  7.36 us
    all_to_all x1, starting transfers between devices, body(): lax.all_to_all(combined, 'tp', split_axis=0, concat_axis=0, tiled=True)  5.84 us
  transfers between devices with their start and end apart: 12, of which 7 were waited for; matrix products, arithmetic and copies ran while one was open for 12% of the time, Pallas kernels for 3%

profile of v2, /device:TPU:2, one launch (start us, length us, event | category | flops | bytes accessed | tf_op | source)
XLA Modules:
  0.0 133.8 jit_solution(887924062002070368)
XLA Ops:
  0.6 0.0 copy-start
  0.6 0.0 copy-start.2
  0.7 0.0 copy-start.1
  0.7 0.0 copy-start.5
  0.7 0.8 copy-done.5
  1.5 0.6 shard_map.111
  2.1 15.2 %all-to-all-start = ((bf16[12,2,1408]{2,1,0:T(2,128)(2,1)}), bf16[12,2,1408]{2,1,0:T(2,128)(2,1)S(1)}, u32[]{:S(2)}, u32[]{:S(2)}) async-start(bf16[12,2,1408]{2,1,0:T(2,128)(2,1)} %shard_map.111), calls=%async_computation | async-start | bytes 135168 | tf_op jit(solution)/shard_map/all_to_all | solution.py:236
  17.3 0.0 copy-start.3
  17.3 0.7 copy-done.3
  18.0 0.0 copy-start.6
  18.0 0.7 copy-done.6
  18.7 0.4 shard_map.110
  19.1 9.3 %all-to-all-done.column_ref = bf16[12,2,1408]{2,1,0:T(2,128)(2,1)S(1)} async-done(((bf16[12,2,1408]{2,1,0:T(2,128)(2,1)}), bf16[12,2,1408]{2,1,0:T(2,128)(2,1)S(1)}, u32[]{:S(2)}, u32[]{:S(2)}) %all-to-all-start) | async-done | bytes 67616 | tf_op jit(solution)/shard_map/all_to_all | solution.py:236
  28.4 1.2 shard_map.112
  29.7 10.6 %all-to-all-start.1 = ((bf16[64,4,1408]{2,1,0:T(4,128)(2,1)}), bf16[64,4,1408]{2,1,0:T(4,128)(2,1)S(1)}, u32[]{:S(2)}, u32[]{:S(2)}) async-start(bf16[64,4,1408]{2,1,0:T(4,128)(2,1)} %shard_map.112), calls=%async_computation.1 | async-start | bytes 1441792 | tf_op jit(solution)/shard_map/all_to_all | solution.py:262
  40.3 0.0 copy-done
  40.3 0.0 copy-done.2
  40.3 0.0 copy-done.1
  40.4 1.2 shard_map.113
  41.6 2.5 %collective-permute-start = (bf16[192,1408]{1,0:T(8,128)(2,1)}, bf16[192,1408]{1,0:T(8,128)(2,1)S(1)}, u32[]{:S(2)}, u32[]{:S(2)}) collective-permute-start(bf16[192,1408]{1,0:T(8,128)(2,1)} %get-tuple-element.38), channel_id=1, source_target_pairs={{0,1},{1,2},{2,3},{3,4},{4,5},{5,6},{6,7},{7,8},{8,9},{9,10},{10,1... | collective-permute-start | bytes 1622024 | tf_op jit(solution)/shard_map/ppermute | solution.py:230
  44.1 4.6 %collective-permute-start.1 = (bf16[192,1408]{1,0:T(8,128)(2,1)}, bf16[192,1408]{1,0:T(8,128)(2,1)S(1)}, u32[]{:S(2)}, u32[]{:S(2)}) collective-permute-start(bf16[192,1408]{1,0:T(8,128)(2,1)} %get-tuple-element.39), channel_id=1, source_target_pairs={{0,11},{1,0},{2,1},{3,2},{4,3},{5,4},{6,5},{7,6},{8,7},{9,8},{10,9... | collective-permute-start | bytes 1622024 | tf_op jit(solution)/shard_map/ppermute | solution.py:230
  48.6 4.0 %reshape_squeeze.3 = bf16[256,4096]{1,0:T(8,128)(2,1)} reshape(bf16[1,64,4,4096]{3,2,1,0:T(4,128)(2,1)} %param.10) | data formatting | bytes 4194304 | tf_op jit(solution)/shard_map/reshape;squeeze | solution.py:264
  52.6 0.0 copy-start.7
  52.6 3.1 %fusion.2 = f32[256,64]{0,1:T(8,128)} fusion(bf16[256,4096]{1,0:T(8,128)(2,1)} %reshape_squeeze.3, bf16[1,4096,64]{1,2,0:T(8,128)(2,1)S(1)} %copy-done), kind=kOutput, calls=%fused_computation.4 | convolution fusion | flops 134217728 | bytes 2686976 | tf_op jit(solution)/shard_map/dot_general | solution.py:266
  55.7 0.0 copy-done.7
  55.7 1.4 %fusion.4 = f32[256,64]{0,1:T(8,128)} fusion(bf16[256,4096]{1,0:T(8,128)(2,1)S(1)} %copy-done.7, bf16[1,4096,64]{1,2,0:T(8,128)(2,1)S(1)} %copy-done.1), kind=kOutput, calls=%fused_computation.6 | convolution fusion | flops 134217728 | bytes 2686976 | tf_op jit(solution)/shard_map/dot_general | solution.py:265
  57.1 5.0 %all-to-all-done.1.got_ref = bf16[64,4,1408]{2,1,0:T(4,128)(2,1)S(1)} async-done(((bf16[64,4,1408]{2,1,0:T(4,128)(2,1)}), bf16[64,4,1408]{2,1,0:T(4,128)(2,1)S(1)}, u32[]{:S(2)}, u32[]{:S(2)}) %all-to-all-start.1) | async-done | bytes 720928 | tf_op jit(solution)/shard_map/all_to_all | solution.py:262
  62.1 0.0 collective-permute-done.low_w_ref
  62.1 0.0 collective-permute-done.1.high_w_ref
  62.1 0.7 shard_map.114
  62.8 2.5 %collective-permute-start.2 = (f32[256,128]{1,0:T(8,128)S(1)}, f32[256,128]{1,0:T(8,128)S(1)}, u32[]{:S(2)}, u32[]{:S(2)}) collective-permute-start(f32[256,128]{1,0:T(8,128)S(1)} %get-tuple-element.41), channel_id=1, source_target_pairs={{0,1},{1,2},{2,3},{3,4},{4,5},{5,6},{6,7},{7,8},{8,9},{9,10},{10,1... | collective-permute-start | bytes 393224 | tf_op jit(solution)/shard_map/ppermute | solution.py:230
  65.3 4.6 %collective-permute-start.3 = (f32[256,128]{1,0:T(8,128)S(1)}, f32[256,128]{1,0:T(8,128)S(1)}, u32[]{:S(2)}, u32[]{:S(2)}) collective-permute-start(f32[256,128]{1,0:T(8,128)S(1)} %get-tuple-element.42), channel_id=1, source_target_pairs={{0,11},{1,0},{2,1},{3,2},{4,3},{5,4},{6,5},{7,6},{8,7},{9,8},{10,9... | collective-permute-start | bytes 393224 | tf_op jit(solution)/shard_map/ppermute | solution.py:230
  69.9 0.9 copy.14.gate_ref
  70.8 0.9 copy.15.up_ref
  71.8 0.0 collective-permute-done.2.low_ref
  71.8 0.6 collective-permute-done.3.high_ref
  72.4 0.3 shard_map.115.own_ref
  72.8 0.0 copy-start.4
  72.8 1.9 %collective-permute-start.4 = (bf16[256,256]{1,0:T(8,128)(2,1)S(1)}, bf16[256,256]{1,0:T(8,128)(2,1)S(1)}, u32[]{:S(2)}, u32[]{:S(2)}) collective-permute-start(bf16[256,256]{1,0:T(8,128)(2,1)S(1)} %shard_map.115.own_ref), channel_id=1, source_target_pairs={{0,1},{1,2},{2,3},{3,4},{4,5},{5,6},{6,7},{7,8},{8,9},{9,10},{10,1... | collective-permute-start | bytes 393224 | tf_op jit(solution)/shard_map/ppermute | solution.py:230
  74.7 5.6 %collective-permute-start.5 = (bf16[256,256]{1,0:T(8,128)(2,1)S(1)}, bf16[256,256]{1,0:T(8,128)(2,1)S(1)}, u32[]{:S(2)}, u32[]{:S(2)}) collective-permute-start(bf16[256,256]{1,0:T(8,128)(2,1)S(1)} %shard_map.115.own_ref), channel_id=1, source_target_pairs={{0,11},{1,0},{2,1},{3,2},{4,3},{5,4},{6,5},{7,6},{8,7},{9,8},{10,9... | collective-permute-start | bytes 393224 | tf_op jit(solution)/shard_map/ppermute | solution.py:230
  80.3 1.0 collective-permute-done.4.low_ref
  81.3 1.5 %collective-permute-done.5.high_ref = bf16[256,256]{1,0:T(8,128)(2,1)S(1)} collective-permute-done((bf16[256,256]{1,0:T(8,128)(2,1)S(1)}, bf16[256,256]{1,0:T(8,128)(2,1)S(1)}, u32[]{:S(2)}, u32[]{:S(2)}) %collective-permute-start.5) | collective-permute-done | bytes 131104 | tf_op jit(solution)/shard_map/ppermute | solution.py:230
  82.8 1.4 %shard_map.116 = bf16[64,4,1408]{2,1,0:T(4,128)(2,1)} custom-call(s32[1]{0:T(128)} %bitcast.part_ref.refs_0_, bf16[256,256]{1,0:T(8,128)(2,1)S(1)} %shard_map.115.own_ref, bf16[256,256]{1,0:T(8,128)(2,1)S(1)} %collective-permute-done.4.low_ref, bf16[256,256]{1,0:T(8,128)(2,1)S(1)} %collective-permute-done.5.high_ref, ...), custom_call_target="tpu_custom_call" | custom-call | flops 276824064 | bytes 720896 | tf_op jit(solution)/shard_map/pallas_call | solution.py:281
  84.2 9.0 %all-to-all-start.2 = ((bf16[64,4,1408]{2,1,0:T(4,128)(2,1)}), bf16[64,4,1408]{2,1,0:T(4,128)(2,1)S(1)}, u32[]{:S(2)}, u32[]{:S(2)}) async-start(bf16[64,4,1408]{2,1,0:T(4,128)(2,1)} %shard_map.116), calls=%async_computation.2 | async-start | bytes 1441792 | tf_op jit(solution)/shard_map/all_to_all | solution.py:291
  93.3 0.0 copy-done.4
  93.3 0.1 copy.12
  93.4 0.4 shard_map.119
  93.8 2.0 %collective-permute-start.6 = (bf16[64,1408]{1,0:T(8,128)(2,1)S(1)}, bf16[64,1408]{1,0:T(8,128)(2,1)S(1)}, u32[]{:S(2)}, u32[]{:S(2)}) collective-permute-start(bf16[64,1408]{1,0:T(8,128)(2,1)S(1)} %get-tuple-element.53), channel_id=1, source_target_pairs={{0,1},{1,2},{2,3},{3,4},{4,5},{5,6},{6,7},{7,8},{8,9},{9,10},{10,1... | collective-permute-start | bytes 540680 | tf_op jit(solution)/shard_map/ppermute | solution.py:230
  95.8 5.5 %collective-permute-start.7 = (bf16[64,1408]{1,0:T(8,128)(2,1)S(1)}, bf16[64,1408]{1,0:T(8,128)(2,1)S(1)}, u32[]{:S(2)}, u32[]{:S(2)}) collective-permute-start(bf16[64,1408]{1,0:T(8,128)(2,1)S(1)} %get-tuple-element.54), channel_id=1, source_target_pairs={{0,11},{1,0},{2,1},{3,2},{4,3},{5,4},{6,5},{7,6},{8,7},{9,8},{10,9... | collective-permute-start | bytes 540680 | tf_op jit(solution)/shard_map/ppermute | solution.py:230
  101.3 3.0 %fusion.1 = bf16[1,4096,64]{1,2,0:T(8,128)(2,1)} fusion(bf16[256,4096]{1,0:T(8,128)(2,1)} %reshape_squeeze.3, bf16[256,256]{1,0:T(8,128)(2,1)S(1)} %shard_map.115.own_ref), kind=kOutput, calls=%fused_computation.3 | convolution fusion | flops 134479872 | bytes 2686976 | tf_op jit(solution)/shard_map/dot_general | solution.py:302
  104.2 10.8 %all-to-all-done.2.refs_3_ = bf16[64,4,1408]{2,1,0:T(4,128)(2,1)S(1)} async-done(((bf16[64,4,1408]{2,1,0:T(4,128)(2,1)}), bf16[64,4,1408]{2,1,0:T(4,128)(2,1)S(1)}, u32[]{:S(2)}, u32[]{:S(2)}) %all-to-all-start.2) | async-done | bytes 720928 | tf_op jit(solution)/shard_map/all_to_all | solution.py:291
  115.0 1.1 shard_map.117
  116.2 5.8 %all-to-all-start.3 = ((bf16[12,2,1408]{2,1,0:T(2,128)(2,1)}), bf16[12,2,1408]{2,1,0:T(2,128)(2,1)S(1)}, u32[]{:S(2)}, u32[]{:S(2)}) async-start(bf16[12,2,1408]{2,1,0:T(2,128)(2,1)} %shard_map.117), calls=%async_computation.3 | async-start | bytes 135168 | tf_op jit(solution)/shard_map/all_to_all | solution.py:321
  122.0 2.9 %fusion = bf16[1,4096,64]{1,2,0:T(8,128)(2,1)} fusion(bf16[256,4096]{1,0:T(8,128)(2,1)} %reshape_squeeze.3, bf16[256,256]{1,0:T(8,128)(2,1)S(1)} %shard_map.115.own_ref), kind=kOutput, calls=%fused_computation.2 | convolution fusion | flops 134479872 | bytes 2686976 | tf_op jit(solution)/shard_map/dot_general | solution.py:299
  124.9 0.0 collective-permute-done.6.low_ref
  124.9 0.0 collective-permute-done.7.high_ref
  124.9 0.9 shard_map.120
  125.8 7.4 %all-to-all-done.3.got_ref = bf16[12,2,1408]{2,1,0:T(2,128)(2,1)S(1)} async-done(((bf16[12,2,1408]{2,1,0:T(2,128)(2,1)}), bf16[12,2,1408]{2,1,0:T(2,128)(2,1)S(1)}, u32[]{:S(2)}, u32[]{:S(2)}) %all-to-all-start.3) | async-done | bytes 67616 | tf_op jit(solution)/shard_map/all_to_all | solution.py:321
  133.1 0.6 shard_map.118
Async XLA Ops:
  0.6 39.7 %copy-start = (bf16[1,4096,64]{1,2,0:T(8,128)(2,1)S(1)}, bf16[1,4096,64]{1,2,0:T(8,128)(2,1)}, u32[]{:S(2)}) copy-start(bf16[1,4096,64]{1,2,0:T(8,128)(2,1)} %param.12) | copy-start | bytes 1572868
  0.6 39.7 %copy-start.2 = (bf16[1,64,4096]{2,1,0:T(8,128)(2,1)S(1)}, bf16[1,64,4096]{2,1,0:T(8,128)(2,1)}, u32[]{:S(2)}) copy-start(bf16[1,64,4096]{2,1,0:T(8,128)(2,1)} %param.13) | copy-start | bytes 1572868
  0.7 39.7 %copy-start.1 = (bf16[1,4096,64]{1,2,0:T(8,128)(2,1)S(1)}, bf16[1,4096,64]{1,2,0:T(8,128)(2,1)}, u32[]{:S(2)}) copy-start(bf16[1,4096,64]{1,2,0:T(8,128)(2,1)} %param.11) | copy-start | bytes 1572868
  0.7 0.8 copy-start.5
  2.1 26.3 %all-to-all-start = ((bf16[12,2,1408]{2,1,0:T(2,128)(2,1)}), bf16[12,2,1408]{2,1,0:T(2,128)(2,1)S(1)}, u32[]{:S(2)}, u32[]{:S(2)}) async-start(bf16[12,2,1408]{2,1,0:T(2,128)(2,1)} %shard_map.111), calls=%async_computation | async-start | bytes 135168 | tf_op jit(solution)/shard_map/all_to_all | solution.py:236
  17.3 0.7 copy-start.3
  18.0 0.7 copy-start.6
  29.7 32.4 %all-to-all-start.1 = ((bf16[64,4,1408]{2,1,0:T(4,128)(2,1)}), bf16[64,4,1408]{2,1,0:T(4,128)(2,1)S(1)}, u32[]{:S(2)}, u32[]{:S(2)}) async-start(bf16[64,4,1408]{2,1,0:T(4,128)(2,1)} %shard_map.112), calls=%async_computation.1 | async-start | bytes 1441792 | tf_op jit(solution)/shard_map/all_to_all | solution.py:262
  41.6 20.5 %collective-permute-start = (bf16[192,1408]{1,0:T(8,128)(2,1)}, bf16[192,1408]{1,0:T(8,128)(2,1)S(1)}, u32[]{:S(2)}, u32[]{:S(2)}) collective-permute-start(bf16[192,1408]{1,0:T(8,128)(2,1)} %get-tuple-element.38), channel_id=1, source_target_pairs={{0,1},{1,2},{2,3},{3,4},{4,5},{5,6},{6,7},{7,8},{8,9},{9,10},{10,1... | collective-permute-start | bytes 1622024 | tf_op jit(solution)/shard_map/ppermute | solution.py:230
  44.1 18.1 %collective-permute-start.1 = (bf16[192,1408]{1,0:T(8,128)(2,1)}, bf16[192,1408]{1,0:T(8,128)(2,1)S(1)}, u32[]{:S(2)}, u32[]{:S(2)}) collective-permute-start(bf16[192,1408]{1,0:T(8,128)(2,1)} %get-tuple-element.39), channel_id=1, source_target_pairs={{0,11},{1,0},{2,1},{3,2},{4,3},{5,4},{6,5},{7,6},{8,7},{9,8},{10,9... | collective-permute-start | bytes 1622024 | tf_op jit(solution)/shard_map/ppermute | solution.py:230
  52.6 3.1 %copy-start.7 = (bf16[256,4096]{1,0:T(8,128)(2,1)S(1)}, bf16[256,4096]{1,0:T(8,128)(2,1)}, u32[]{:S(2)}) copy-start(bf16[256,4096]{1,0:T(8,128)(2,1)} %reshape_squeeze.3) | copy-start | bytes 6291460
  62.8 8.9 %collective-permute-start.2 = (f32[256,128]{1,0:T(8,128)S(1)}, f32[256,128]{1,0:T(8,128)S(1)}, u32[]{:S(2)}, u32[]{:S(2)}) collective-permute-start(f32[256,128]{1,0:T(8,128)S(1)} %get-tuple-element.41), channel_id=1, source_target_pairs={{0,1},{1,2},{2,3},{3,4},{4,5},{5,6},{6,7},{7,8},{8,9},{9,10},{10,1... | collective-permute-start | bytes 393224 | tf_op jit(solution)/shard_map/ppermute | solution.py:230
  65.3 7.1 %collective-permute-start.3 = (f32[256,128]{1,0:T(8,128)S(1)}, f32[256,128]{1,0:T(8,128)S(1)}, u32[]{:S(2)}, u32[]{:S(2)}) collective-permute-start(f32[256,128]{1,0:T(8,128)S(1)} %get-tuple-element.42), channel_id=1, source_target_pairs={{0,11},{1,0},{2,1},{3,2},{4,3},{5,4},{6,5},{7,6},{8,7},{9,8},{10,9... | collective-permute-start | bytes 393224 | tf_op jit(solution)/shard_map/ppermute | solution.py:230
  72.8 20.5 %copy-start.4 = (s32[1,24,8]{1,2,0:T(8,128)S(1)}, s32[1,24,8]{1,2,0:T(8,128)}, u32[]{:S(2)}) copy-start(s32[1,24,8]{1,2,0:T(8,128)} %param.9) | copy-start | bytes 2308
  72.8 8.5 %collective-permute-start.4 = (bf16[256,256]{1,0:T(8,128)(2,1)S(1)}, bf16[256,256]{1,0:T(8,128)(2,1)S(1)}, u32[]{:S(2)}, u32[]{:S(2)}) collective-permute-start(bf16[256,256]{1,0:T(8,128)(2,1)S(1)} %shard_map.115.own_ref), channel_id=1, source_target_pairs={{0,1},{1,2},{2,3},{3,4},{4,5},{5,6},{6,7},{7,8},{8,9},{9,10},{10,1... | collective-permute-start | bytes 393224 | tf_op jit(solution)/shard_map/ppermute | solution.py:230
  74.7 8.1 %collective-permute-start.5 = (bf16[256,256]{1,0:T(8,128)(2,1)S(1)}, bf16[256,256]{1,0:T(8,128)(2,1)S(1)}, u32[]{:S(2)}, u32[]{:S(2)}) collective-permute-start(bf16[256,256]{1,0:T(8,128)(2,1)S(1)} %shard_map.115.own_ref), channel_id=1, source_target_pairs={{0,11},{1,0},{2,1},{3,2},{4,3},{5,4},{6,5},{7,6},{8,7},{9,8},{10,9... | collective-permute-start | bytes 393224 | tf_op jit(solution)/shard_map/ppermute | solution.py:230
  84.2 30.8 %all-to-all-start.2 = ((bf16[64,4,1408]{2,1,0:T(4,128)(2,1)}), bf16[64,4,1408]{2,1,0:T(4,128)(2,1)S(1)}, u32[]{:S(2)}, u32[]{:S(2)}) async-start(bf16[64,4,1408]{2,1,0:T(4,128)(2,1)} %shard_map.116), calls=%async_computation.2 | async-start | bytes 1441792 | tf_op jit(solution)/shard_map/all_to_all | solution.py:291
  93.8 31.1 %collective-permute-start.6 = (bf16[64,1408]{1,0:T(8,128)(2,1)S(1)}, bf16[64,1408]{1,0:T(8,128)(2,1)S(1)}, u32[]{:S(2)}, u32[]{:S(2)}) collective-permute-start(bf16[64,1408]{1,0:T(8,128)(2,1)S(1)} %get-tuple-element.53), channel_id=1, source_target_pairs={{0,1},{1,2},{2,3},{3,4},{4,5},{5,6},{6,7},{7,8},{8,9},{9,10},{10,1... | collective-permute-start | bytes 540680 | tf_op jit(solution)/shard_map/ppermute | solution.py:230
  95.8 29.1 %collective-permute-start.7 = (bf16[64,1408]{1,0:T(8,128)(2,1)S(1)}, bf16[64,1408]{1,0:T(8,128)(2,1)S(1)}, u32[]{:S(2)}, u32[]{:S(2)}) collective-permute-start(bf16[64,1408]{1,0:T(8,128)(2,1)S(1)} %get-tuple-element.54), channel_id=1, source_target_pairs={{0,11},{1,0},{2,1},{3,2},{4,3},{5,4},{6,5},{7,6},{8,7},{9,8},{10,9... | collective-permute-start | bytes 540680 | tf_op jit(solution)/shard_map/ppermute | solution.py:230
  116.2 17.0 %all-to-all-start.3 = ((bf16[12,2,1408]{2,1,0:T(2,128)(2,1)}), bf16[12,2,1408]{2,1,0:T(2,128)(2,1)S(1)}, u32[]{:S(2)}, u32[]{:S(2)}) async-start(bf16[12,2,1408]{2,1,0:T(2,128)(2,1)} %shard_map.117), calls=%async_computation.3 | async-start | bytes 135168 | tf_op jit(solution)/shard_map/all_to_all | solution.py:321

commit v3 on v2

--- a/solution.py
+++ b/solution.py
@@ -7,9 +7,12 @@
 
 PARTS = 3
 LANES = 128
+WEIGHT_ROWS = 16
 F32, BF16 = jnp.float32, jnp.bfloat16
 COLUMN = ("dp", "ctx")
 VMEM = pl.BlockSpec(memory_space=pltpu.VMEM)
+NT = (((1,), (1,)), ((), ()))
+TN = (((0,), (0,)), ((), ()))
 SMEM = pl.BlockSpec(memory_space=pltpu.SMEM)
 
 
@@ -67,16 +70,46 @@
             out_ref[peer] = piece
 
 
-def weights_kernel(part_ref, gate_ref, up_ref, down_ref, own_ref, high_ref, low_ref, stage_ref):
+def neighbours(part):
+    return lax.rem(part + 1, PARTS), lax.rem(part + PARTS - 1, PARTS)
+
+
+def strip(place, width):
+    return pl.ds(pl.multiple_of(place * width, LANES), width)
+
+
+def weights_kernel(
+    part_ref, gate_ref, up_ref, down_ref,
+    own_ref, high_ref, low_ref, own_down_ref, high_down_ref, low_down_ref, stage_ref,
+):
     units, model = gate_ref.shape
     width = own_ref.shape[1]
     part = part_ref[0]
-    above, below = lax.rem(part + 1, PARTS), lax.rem(part + PARTS - 1, PARTS)
+    above, below = neighbours(part)
     for at, ref in enumerate((gate_ref, up_ref, down_ref)):
         stage_ref[at * units : (at + 1) * units, :model] = ref[...]
-    stage_ref[:, model:] = jnp.zeros((PARTS * units, PARTS * width - model), BF16)
-    for ref, place in ((own_ref, part), (high_ref, above), (low_ref, below)):
-        ref[...] = stage_ref[:, pl.ds(pl.multiple_of(place * width, LANES), width)]
+    stage_ref[:, model:] = jnp.zeros((3 * units, PARTS * width - model), BF16)
+    for ref, down_out_ref, place in (
+        (own_ref, own_down_ref, part),
+        (high_ref, high_down_ref, above),
+        (low_ref, low_down_ref, below),
+    ):
+        ref[...] = stage_ref[: 2 * units, strip(place, width)]
+        down_out_ref[...] = stage_ref[2 * units :, strip(place, width)]
+
+
+def factors_kernel(gate_ref, up_ref, out_ref):
+    gate_pre, up_pre = gate_ref[...], up_ref[...]
+    sigmoid = jax.nn.sigmoid(gate_pre)
+    activated = gate_pre * sigmoid
+    out_ref[...] = jnp.concatenate(
+        [
+            up_pre * sigmoid * (1.0 + gate_pre * (1.0 - sigmoid)),
+            activated,
+            activated * up_pre,
+        ],
+        axis=0,
+    )
 
 
 def send_kernel(part_ref, pick_ref, column_ref, out_ref):
@@ -93,67 +126,66 @@
     out_ref[...] = rows.reshape(experts, cap, width).astype(BF16)
 
 
-def upward_kernel(part_ref, got_ref, own_w_ref, low_w_ref, high_w_ref, rows_ref, own_ref, to_low_ref, to_high_ref):
+def upward_kernel(part_ref, got_ref, own_ref, low_ref, high_ref, factors_ref, rows_ref, out_ref):
     experts, cap, width = got_ref.shape
-    slots, units = experts * cap, own_w_ref.shape[0] // 3
+    slots, units = experts * cap, own_ref.shape[0]
     rows = got_ref[...].reshape(slots, width)
     rows_ref[...] = rows
-    nt = (((1,), (1,)), ((), ()))
-    weight = jnp.where(
-        part_ref[0] == PARTS - 1, rows[:, width - LANES : width - LANES + units].astype(F32), 0.0
-    )
-    for w_ref, ref in ((own_w_ref, own_ref), (low_w_ref, to_low_ref), (high_w_ref, to_high_ref)):
-        product = lax.dot_general(rows, w_ref[2 * units :], nt, preferred_element_type=F32)
-        ref[...] = jnp.concatenate([product, weight], axis=1)
-
-
-def expert_kernel(own_ref, low_ref, high_ref, gate_ref, up_ref, out_ref):
-    slots, units = gate_ref.shape
-    total = own_ref[...] + low_ref[...] + high_ref[...]
-    upward, weight = total[:, :units], total[:, units:]
-    gate_pre, up_pre = gate_ref[...], up_ref[...]
-    sigmoid = jax.nn.sigmoid(gate_pre)
-    activated = gate_pre * sigmoid
-    hidden = activated * up_pre
-    part_prob = jnp.sum(hidden * upward, axis=1, keepdims=True)
-    hidden_grad = weight * upward
-    gate_grad = hidden_grad * up_pre * sigmoid * (1.0 + gate_pre * (1.0 - sigmoid))
-    up_grad = hidden_grad * activated
-    lane = lax.broadcasted_iota(jnp.int32, (slots, units), 1)
-    high = part_prob.astype(BF16).astype(F32)
-    prob = jnp.where(lane == 0, high, part_prob - high)
-    both = jnp.concatenate([gate_grad, up_grad], axis=1)
-    rest = jnp.concatenate([hidden * weight, prob], axis=1)
-    out_ref[...] = jnp.concatenate([both, rest], axis=1).astype(BF16)
-
-
-def back_kernel(part_ref, own_ref, low_ref, high_ref, own_w_ref, low_w_ref, high_w_ref, out_ref):
+    part = part_ref[0]
+    above, below = neighbours(part)
+    for ref, place in ((own_ref, part), (low_ref, below), (high_ref, above)):
+        product = lax.dot_general(ref[...], rows, NT, preferred_element_type=F32)
+        out_ref[pl.ds(pl.multiple_of(place * units, units), units)] = product.astype(BF16)
+    weight = rows[:, width - LANES :].astype(F32).T[:WEIGHT_ROWS]
+    low = 3 * units + WEIGHT_ROWS
+    out_ref[3 * units : low] = jnp.where(part == PARTS - 1, weight, 0.0).astype(BF16)
+    out_ref[low:] = factors_ref[...].astype(BF16)
+
+
+def expert_kernel(
+    part_ref, all_ref, own_ref, own_w_ref, low_w_ref, high_w_ref,
+    out_ref, terms_ref, hidden_ref, total_ref,
+):
     experts, cap, width = out_ref.shape
-    slots, units = own_ref.shape[0], own_ref.shape[1] // 4
-    pairs = ((own_ref, own_w_ref), (low_ref, low_w_ref), (high_ref, high_w_ref))
-    left = jnp.concatenate([ref[:, : 2 * units] for ref, _ in pairs], axis=1)
-    right = jnp.concatenate([ref[: 2 * units] for _, ref in pairs], axis=0)
-    grads = jnp.dot(left, right, preferred_element_type=F32)
-    prob = jnp.zeros((slots, 1), F32)
-    for ref, _ in pairs:
-        prob = prob + jnp.sum(
-            ref[:, 2 * units :].astype(F32)[:, units : units + 2], axis=1, keepdims=True
-        )
+    slots = experts * cap
+    units = own_ref.shape[0] // 3
+    part = part_ref[0]
+    above, below = neighbours(part)
+    first = total_ref.shape[0]
+    total = all_ref[0, :first].astype(F32)
+    for peer in range(1, PARTS):
+        total = total + all_ref[peer, :first].astype(F32)
+    total_ref[...] = total
+    weight = total[3 * units : 3 * units + 1]
+    prob = jnp.zeros((1, slots), F32)
+    left, scaled = [], []
+    right = [own_w_ref[...], low_w_ref[...], high_w_ref[...]]
+    for place in (part, below, above):
+        upward = total_ref[pl.ds(pl.multiple_of(place * units, units), units)]
+        if place is part:
+            factors = own_ref[...]
+        else:
+            factors = all_ref[place, first:].astype(F32)
+        by_gate, by_up, hidden = (factors[at * units : (at + 1) * units] for at in range(3))
+        prob = prob + jnp.sum(hidden * upward, axis=0, keepdims=True)
+        hidden_grad = weight * upward
+        left += [hidden_grad * by_gate, hidden_grad * by_up]
+        scaled.append(hidden * weight)
+    left = jnp.concatenate(left, axis=0).astype(BF16)
+    terms_ref[...] = left[: 2 * units]
+    hidden_ref[...] = jnp.concatenate(scaled, axis=0).astype(BF16)
+    grads = lax.dot_general(left, jnp.concatenate(right, axis=0), TN, preferred_element_type=F32)
+    lane = lax.broadcasted_iota(jnp.int32, (LANES, slots), 0)
     high = prob.astype(BF16).astype(F32)
-    lane = lax.broadcasted_iota(jnp.int32, (slots, LANES), 1)
-    prob = jnp.where(lane == 0, high, prob - high)
-    last = jnp.where(part_ref[0] == PARTS - 1, prob, grads[:, width - LANES :])
+    prob = jnp.where(lane == 0, high, jnp.where(lane == 1, prob - high, 0.0)).T
+    last = jnp.where(part == PARTS - 1, prob, grads[:, width - LANES :])
     grads = jnp.concatenate([grads[:, : width - LANES], last], axis=1)
     out_ref[...] = grads.reshape(experts, cap, width).astype(BF16)
 
 
-def down_kernel(rows_ref, own_ref, low_ref, high_ref, own_out_ref, low_out_ref, high_out_ref):
-    units = own_ref.shape[1] // 4
-    tn = (((0,), (0,)), ((), ()))
-    left = jnp.concatenate(
-        [ref[:, 2 * units : 3 * units] for ref in (own_ref, low_ref, high_ref)], axis=1
-    )
-    grads = lax.dot_general(left, rows_ref[...], tn, preferred_element_type=F32).astype(BF16)
+def down_kernel(rows_ref, hidden_ref, own_out_ref, low_out_ref, high_out_ref):
+    units = own_out_ref.shape[0]
+    grads = jnp.dot(hidden_ref[...], rows_ref[...], preferred_element_type=F32).astype(BF16)
     for at, ref in enumerate((own_out_ref, low_out_ref, high_out_ref)):
         ref[...] = grads[at * units : (at + 1) * units]
 
@@ -161,9 +193,9 @@
 def join_kernel(part_ref, own_ref, low_ref, high_ref, out_ref, stage_ref):
     units, width = own_ref.shape
     part = part_ref[0]
-    above, below = lax.rem(part + 1, PARTS), lax.rem(part + PARTS - 1, PARTS)
+    above, below = neighbours(part)
     for ref, place in ((own_ref, part), (low_ref, below), (high_ref, above)):
-        stage_ref[:, pl.ds(pl.multiple_of(place * width, LANES), width)] = ref[...]
+        stage_ref[:, strip(place, width)] = ref[...]
     out_ref[...] = stage_ref[:, : out_ref.shape[1]]
 
 
@@ -224,9 +256,11 @@
     def shape(*dims, dtype=BF16):
         return jax.ShapeDtypeStruct(dims, dtype)
 
+    groups = [list(range(at, at + PARTS)) for at in range(0, tp_count, PARTS)]
+
     def trade(to_low, to_high):
-        rise = [(i, (i + 1) % tp_count) for i in range(tp_count)]
-        fall = [(i, (i - 1) % tp_count) for i in range(tp_count)]
+        rise = [(g[i], g[(i + 1) % PARTS]) for g in groups for i in range(PARTS)]
+        fall = [(g[(i + 1) % PARTS], g[i]) for g in groups for i in range(PARTS)]
         return lax.ppermute(to_high, "tp", rise), lax.ppermute(to_low, "tp", fall)
 
     thirds = call(thirds_kernel, shape(tp_count, own, width), [VMEM], 0, 100000)(grad_out[0])
@@ -242,16 +276,20 @@
         1000000,
         100000,
     )(ids.T, probs[0].T)
-    slab = shape(3 * units, width)
-    own_w, to_high_w, to_low_w = call(
+    slab, thin = shape(2 * units, width), shape(units, width)
+    own_w, high_w, low_w, own_down, high_down, low_down = call(
         weights_kernel,
-        [slab, slab, slab],
+        [slab] * 3 + [thin] * 3,
         [SMEM] + [VMEM] * 3,
         0,
         12 * units * model,
         (pltpu.VMEM((3 * units, PARTS * width), BF16),),
     )(part, gate_rows, up_rows, down_rows)
-    low_w, high_w = trade(to_low_w, to_high_w)
+    pick, high_w, low_w, high_down, low_down = lax.optimization_barrier(
+        (pick, high_w, low_w, high_down, low_down)
+    )
+    from_low_down, from_high_down = trade(low_down, high_down)
+    from_low_w, from_high_w = trade(low_w, high_w)
     sent = call(
         send_kernel,
         shape(experts, cap, width),
@@ -262,46 +300,41 @@
     mine = lax.all_to_all(sent, COLUMN, split_axis=0, concat_axis=0, tiled=True)
 
     rows_input = saved_inputs[0].reshape(slots, model)
-    gate_pre = jnp.dot(rows_input, w_gate[0], preferred_element_type=F32)
-    up_pre = jnp.dot(rows_input, w_up[0], preferred_element_type=F32)
-    mine, gate_pre, up_pre = lax.optimization_barrier((mine, gate_pre, up_pre))
-    wide_sum = shape(slots, 2 * units, dtype=F32)
-    rows, up_own, up_to_low, up_to_high = call(
+    gate_pre = lax.dot_general(gate_rows, rows_input, NT, preferred_element_type=F32)
+    up_pre = lax.dot_general(up_rows, rows_input, NT, preferred_element_type=F32)
+    factors = call(
+        factors_kernel,
+        shape(3 * units, slots, dtype=F32),
+        [VMEM] * 2,
+        20 * slots * units,
+        20 * slots * units,
+    )(gate_pre, up_pre)
+    rows, partial = call(
         upward_kernel,
-        [shape(slots, width), wide_sum, wide_sum, wide_sum],
-        [SMEM] + [VMEM] * 4,
+        [shape(slots, width), shape(6 * units + WEIGHT_ROWS, slots)],
+        [SMEM] + [VMEM] * 5,
         6 * slots * width * units,
         4 * slots * width,
-    )(part, mine, own_w, low_w, high_w)
-    up_low, up_high = trade(up_to_low, up_to_high)
-    terms = call(
-        expert_kernel, shape(slots, 4 * units), [VMEM] * 5, 20 * slots * units, 20 * slots * units
-    )(up_own, up_low, up_high, gate_pre, up_pre)
-    low_terms, high_terms = trade(terms, terms)
-    summed = call(
-        back_kernel,
-        shape(experts, cap, width),
-        [SMEM] + [VMEM] * 6,
+    )(part, mine, own_down, from_low_down, from_high_down, factors)
+    partials = lax.all_gather(partial, "tp", axis=0, axis_index_groups=groups)
+    summed, terms, hidden = call(
+        expert_kernel,
+        [shape(experts, cap, width), shape(2 * units, slots), shape(3 * units, slots)],
+        [SMEM] + [VMEM] * 5,
         12 * slots * width * units,
         2 * slots * width,
-    )(part, terms, low_terms, high_terms, own_w, low_w, high_w)
-    summed, terms, low_terms, high_terms = lax.optimization_barrier(
-        (summed, terms, low_terms, high_terms)
-    )
+        (pltpu.VMEM((3 * units + WEIGHT_ROWS, slots), F32),),
+    )(part, partials, factors, own_w, from_low_w, from_high_w)
+    summed, terms, hidden = lax.optimization_barrier((summed, terms, hidden))
     got = lax.all_to_all(summed, COLUMN, split_axis=0, concat_axis=0, tiled=True)
 
-    tn = (((0,), (0,)), ((), ()))
-    strip = shape(units, width)
     down_own, down_to_low, down_to_high = call(
-        down_kernel, [strip] * 3, [VMEM] * 4, 6 * slots * units * width, 2 * slots * width
-    )(rows, terms, low_terms, high_terms)
+        down_kernel, [thin] * 3, [VMEM] * 2, 6 * slots * units * width, 2 * slots * width
+    )(rows, hidden)
     down_low, down_high = trade(down_to_low, down_to_high)
-    grad_gate = lax.dot_general(
-        rows_input, terms[:, :units], tn, preferred_element_type=F32
-    )
-    grad_up = lax.dot_general(
-        rows_input, terms[:, units : 2 * units], tn, preferred_element_type=F32
-    )
+    grad_gate = jnp.dot(terms[:units], rows_input, preferred_element_type=F32).astype(BF16)
+    grad_up = jnp.dot(terms[units:], rows_input, preferred_element_type=F32).astype(BF16)
+    got, grad_gate, down_own = lax.optimization_barrier((got, grad_gate, down_own))
     grad_down = call(
         join_kernel,
         shape(units, model),
@@ -310,7 +343,6 @@
         4 * units * model,
         (pltpu.VMEM((units, PARTS * width), BF16),),
     )(part, down_own, down_low, down_high)
-
     combined = call(
         lambda *refs: combine_kernel(cap, *refs),
         shape(tp_count, own, width),
@@ -329,8 +361,8 @@
     return (
         grad_tokens[None],
         grad_probs[None],
-        grad_gate.astype(BF16)[None],
-        grad_up.astype(BF16)[None],
+        grad_gate.T[None],
+        grad_up.T[None],
         grad_down[None],
     )
 

time: 135 us -> 131 us (0.970)
  blocking collectives: 0 us -> 15.1 us
  waiting for transfers between devices: 35.6 us -> 25.1 us
  starting transfers between devices: 69.8 us -> 62.1 us
  matrix products: 10.4 us -> 8.99 us
    all_gather x0 -> x1, blocking collectives: none -> 15.1 us  [body(): partials = lax.all_gather(partial, 'tp', axis=0, axis_index_groups=groups)]
    ppermute x8 -> x6, starting transfers between devices: 29.1 us -> 20.4 us  [trade(): return (lax.ppermute(to_high, 'tp', rise), lax.ppermute(to_low, 'tp', fall))]
    all_to_all x1, waiting for transfers between devices: 9.34 us -> 5.13 us  [body(): lax.all_to_all(thirds, 'tp', split_axis=0, concat_axis=0, tiled=True)]
    all_to_all x1, waiting for transfers between devices: 4.96 us -> 0.79 us  [body(): mine = lax.all_to_all(sent, COLUMN, split_axis=0, concat_axis=0, tiled=True)]
    ppermute x8 -> x6, waiting for transfers between devices: 3.12 us -> 0.02 us  [trade(): return (lax.ppermute(to_high, 'tp', rise), lax.ppermute(to_low, 'tp', fall))]
    unnamed x17 -> x21, local copies, waits for them, and re-layouts: 2.28 us -> 5.29 us
    optimization_barrier x2 -> x0, local copies, waits for them, and re-layouts: 1.87 us -> none  [body(): mine, gate_pre, up_pre = lax.optimization_barrier((mine, gate_pre, up_pre))]
    dot_general x4, matrix products: 10.4 us -> 8.99 us  [the longest x1 2.87 us: body(): jnp.dot(terms[:units], rows_input, preferred_element_type=F32).astype(BF16)]
  transfers between devices with their start and end apart: 12 -> 10, of which waited for: 7 -> 4; matrix products, arithmetic and copies ran while one was open for 12% -> 10% of each run, Pallas kernels for 3% -> 4%
where the time goes in v3:
time: 131 us; the launch traced here: 130 us
  starting transfers between devices  62.1 us (47%)
  waiting for transfers between devices  25.1 us (19%)
  blocking collectives  15.1 us (12%)
  local copies, waits for them, and re-layouts  9.26 us (7%)
  matrix products  8.99 us (7%)
  Pallas kernels  8.65 us (7%)
    ppermute x6, starting transfers between devices, trade(): return (lax.ppermute(to_high, 'tp', rise), lax.ppermute(to_low, 'tp', fall))  20.4 us
    all_to_all x1, starting transfers between devices, body(): lax.all_to_all(thirds, 'tp', split_axis=0, concat_axis=0, tiled=True)  15.2 us
    all_gather x1, blocking collectives, body(): partials = lax.all_gather(partial, 'tp', axis=0, axis_index_groups=groups)  15.1 us
    all_to_all x1, waiting for transfers between devices, body(): lax.all_to_all(summed, COLUMN, split_axis=0, concat_axis=0, tiled=True)  11.7 us
    all_to_all x1, starting transfers between devices, body(): mine = lax.all_to_all(sent, COLUMN, split_axis=0, concat_axis=0, tiled=True)  10.7 us
    all_to_all x1, starting transfers between devices, body(): lax.all_to_all(summed, COLUMN, split_axis=0, concat_axis=0, tiled=True)  10.3 us
    all_to_all x1, waiting for transfers between devices, body(): lax.all_to_all(combined, 'tp', split_axis=0, concat_axis=0, tiled=True)  7.38 us
    all_to_all x1, starting transfers between devices, body(): lax.all_to_all(combined, 'tp', split_axis=0, concat_axis=0, tiled=True)  5.67 us
  transfers between devices with their start and end apart: 10, of which 4 were waited for; matrix products, arithmetic and copies ran while one was open for 10% of the time, Pallas kernels for 4%

profile of v3, /device:TPU:2, one launch (start us, length us, event | category | flops | bytes accessed | tf_op | source)
XLA Modules:
  0.0 130.0 jit_solution(5781105432391345555)
XLA Ops:
  0.6 0.0 copy-start.7
  0.6 0.7 copy-done.7
  1.3 0.6 shard_map.111
  2.0 15.2 %all-to-all-start = ((bf16[12,2,1408]{2,1,0:T(2,128)(2,1)}), bf16[12,2,1408]{2,1,0:T(2,128)(2,1)S(1)}, u32[]{:S(2)}, u32[]{:S(2)}) async-start(bf16[12,2,1408]{2,1,0:T(2,128)(2,1)} %shard_map.111), calls=%async_computation | async-start | bytes 135168 | tf_op jit(solution)/shard_map/all_to_all | solution.py:270
  17.2 0.0 copy-start
  17.2 1.0 copy-done
  18.2 0.0 copy-start.2
  18.2 1.0 copy-done.2
  19.3 0.0 copy-start.4
  19.3 1.0 copy-done.4
  20.3 1.1 shard_map.112
  21.4 0.0 copy-start.5
  21.4 0.7 copy-done.5
  22.1 0.0 copy-start.8
  22.1 0.7 copy-done.8
  22.8 0.4 shard_map.110
  23.2 5.1 %all-to-all-done.column_ref = bf16[12,2,1408]{2,1,0:T(2,128)(2,1)S(1)} async-done(((bf16[12,2,1408]{2,1,0:T(2,128)(2,1)}), bf16[12,2,1408]{2,1,0:T(2,128)(2,1)S(1)}, u32[]{:S(2)}, u32[]{:S(2)}) %all-to-all-start) | async-done | bytes 67616 | tf_op jit(solution)/shard_map/all_to_all | solution.py:270
  28.3 1.2 shard_map.113
  29.5 10.7 %all-to-all-start.1 = ((bf16[64,4,1408]{2,1,0:T(4,128)(2,1)}), bf16[64,4,1408]{2,1,0:T(4,128)(2,1)S(1)}, u32[]{:S(2)}, u32[]{:S(2)}) async-start(bf16[64,4,1408]{2,1,0:T(4,128)(2,1)} %shard_map.113), calls=%async_computation.1 | async-start | bytes 1441792 | tf_op jit(solution)/shard_map/all_to_all | solution.py:300
  40.2 0.0 copy-start.1
  40.2 2.6 %collective-permute-start = (bf16[64,1408]{1,0:T(8,128)(2,1)S(1)}, bf16[64,1408]{1,0:T(8,128)(2,1)S(1)}, u32[]{:S(2)}, u32[]{:S(2)}) collective-permute-start(bf16[64,1408]{1,0:T(8,128)(2,1)S(1)} %get-tuple-element.47), channel_id=1, source_target_pairs={{0,1},{1,2},{2,0},{3,4},{4,5},{5,3},{6,7},{7,8},{8,6},{9,10},{10,1... | collective-permute-start | bytes 540680 | tf_op jit(solution)/shard_map/ppermute | solution.py:264
  42.8 4.3 %collective-permute-start.1 = (bf16[64,1408]{1,0:T(8,128)(2,1)S(1)}, bf16[64,1408]{1,0:T(8,128)(2,1)S(1)}, u32[]{:S(2)}, u32[]{:S(2)}) collective-permute-start(bf16[64,1408]{1,0:T(8,128)(2,1)S(1)} %get-tuple-element.48), channel_id=1, source_target_pairs={{1,0},{2,1},{0,2},{4,3},{5,4},{3,5},{7,6},{8,7},{6,8},{10,9},{11,1... | collective-permute-start | bytes 540680 | tf_op jit(solution)/shard_map/ppermute | solution.py:264
  47.1 1.9 %collective-permute-start.2 = (bf16[128,1408]{1,0:T(8,128)(2,1)}, bf16[128,1408]{1,0:T(8,128)(2,1)S(1)}, u32[]{:S(2)}, u32[]{:S(2)}) collective-permute-start(bf16[128,1408]{1,0:T(8,128)(2,1)} %get-tuple-element.51), channel_id=1, source_target_pairs={{0,1},{1,2},{2,0},{3,4},{4,5},{5,3},{6,7},{7,8},{8,6},{9,10},{10,1... | collective-permute-start | bytes 1081352 | tf_op jit(solution)/shard_map/ppermute | solution.py:264
  49.0 4.8 %collective-permute-start.3 = (bf16[128,1408]{1,0:T(8,128)(2,1)}, bf16[128,1408]{1,0:T(8,128)(2,1)S(1)}, u32[]{:S(2)}, u32[]{:S(2)}) collective-permute-start(bf16[128,1408]{1,0:T(8,128)(2,1)} %get-tuple-element.52), channel_id=1, source_target_pairs={{1,0},{2,1},{0,2},{4,3},{5,4},{3,5},{7,6},{8,7},{6,8},{10,9},{11,1... | collective-permute-start | bytes 1081352 | tf_op jit(solution)/shard_map/ppermute | solution.py:264
  53.8 4.0 %reshape_squeeze.3 = bf16[256,4096]{1,0:T(8,128)(2,1)} reshape(bf16[1,64,4,4096]{3,2,1,0:T(4,128)(2,1)} %param.10) | data formatting | bytes 4194304 | tf_op jit(solution)/shard_map/reshape;squeeze | solution.py:302
  57.8 0.0 copy-done.1
  57.8 0.0 copy-start.3
  57.8 0.0 copy-start.9
  57.8 2.5 %fusion.3.gate_ref = f32[64,256]{1,0:T(8,128)S(1)} fusion(bf16[64,4096]{1,0:T(8,128)(2,1)S(1)} %bitcast.34, bf16[256,4096]{1,0:T(8,128)(2,1)} %reshape_squeeze.3), kind=kOutput, calls=%fused_computation.5 | convolution fusion | flops 134217728 | bytes 2686976 | tf_op jit(solution)/shard_map/dot_general | solution.py:303
  60.3 0.0 copy-done.3
  60.3 0.0 copy-done.9
  60.3 0.8 fusion.4.up_ref
  61.1 0.0 collective-permute-done.low_ref
  61.2 0.0 collective-permute-done.1.high_ref
  61.2 0.8 all-to-all-done.1.got_ref
  62.0 0.8 shard_map.115
  62.7 0.0 copy-start.6
  62.8 15.1 %all-gather = bf16[1200,256]{1,0:T(8,128)(2,1)S(1)} all-gather(bf16[400,256]{1,0:T(8,128)(2,1)S(1)} %get-tuple-element.49), channel_id=2, replica_groups={{0,1,2},{3,4,5},{6,7,8},{9,10,11},{12,13,14},{15,16,17},{18,19,20},{21,..., dimensions={0}, use_global_device_ids=true | all-gather | bytes 819200 | tf_op jit(solution)/shard_map/all_gather | solution.py:319
  77.8 0.0 collective-permute-done.2.low_w_ref
  77.8 0.0 collective-permute-done.3.high_w_ref
  77.8 1.5 %shard_map.116 = (bf16[64,4,1408]{2,1,0:T(4,128)(2,1)}, bf16[128,256]{1,0:T(8,128)(2,1)S(1)}, bf16[192,256]{1,0:T(8,128)(2,1)S(1)}) custom-call(s32[1]{0:T(128)} %bitcast.part_ref.refs_0_, bf16[3,400,256]{2,1,0:T(8,128)(2,1)S(1)} %bitcast.32, f32[192,256]{1,0:T(8,128)S(1)} %shard_map.114.factors_ref.own_ref, ...), custom_call_target="tpu_custom_call" | custom-call | flops 276824064 | bytes 720896 | tf_op jit(solution)/shard_map/pallas_call | solution.py:320
  79.3 10.3 %all-to-all-start.2 = ((bf16[64,4,1408]{2,1,0:T(4,128)(2,1)}), bf16[64,4,1408]{2,1,0:T(4,128)(2,1)S(1)}, u32[]{:S(2)}, u32[]{:S(2)}) async-start(bf16[64,4,1408]{2,1,0:T(4,128)(2,1)} %get-tuple-element.53), calls=%async_computation.2 | async-start | bytes 1441792 | tf_op jit(solution)/shard_map/all_to_all | solution.py:329
  89.7 0.0 copy-done.6
  89.7 0.1 copy.12
  89.7 0.3 shard_map.117
  90.1 2.5 %collective-permute-start.4 = (bf16[64,1408]{1,0:T(8,128)(2,1)S(1)}, bf16[64,1408]{1,0:T(8,128)(2,1)S(1)}, u32[]{:S(2)}, u32[]{:S(2)}) collective-permute-start(bf16[64,1408]{1,0:T(8,128)(2,1)S(1)} %get-tuple-element.63), channel_id=1, source_target_pairs={{0,1},{1,2},{2,0},{3,4},{4,5},{5,3},{6,7},{7,8},{8,6},{9,10},{10,1... | collective-permute-start | bytes 540680 | tf_op jit(solution)/shard_map/ppermute | solution.py:264
  92.6 4.2 %collective-permute-start.5 = (bf16[64,1408]{1,0:T(8,128)(2,1)S(1)}, bf16[64,1408]{1,0:T(8,128)(2,1)S(1)}, u32[]{:S(2)}, u32[]{:S(2)}) collective-permute-start(bf16[64,1408]{1,0:T(8,128)(2,1)S(1)} %get-tuple-element.64), channel_id=1, source_target_pairs={{1,0},{2,1},{0,2},{4,3},{5,4},{3,5},{7,6},{8,7},{6,8},{10,9},{11,1... | collective-permute-start | bytes 540680 | tf_op jit(solution)/shard_map/ppermute | solution.py:264
  96.8 2.9 %convolution_convert_fusion.1 = bf16[64,4096]{1,0:T(8,128)(2,1)} fusion(bf16[256,4096]{1,0:T(8,128)(2,1)} %reshape_squeeze.3, bf16[128,256]{1,0:T(8,128)(2,1)S(1)} %get-tuple-element.54), kind=kOutput, calls=%fused_computation.1 | convolution fusion | flops 134479872 | bytes 2654208 | tf_op jit(solution)/shard_map/dot_general | solution.py:335
  99.7 11.7 %all-to-all-done.2.refs_3_ = bf16[64,4,1408]{2,1,0:T(4,128)(2,1)S(1)} async-done(((bf16[64,4,1408]{2,1,0:T(4,128)(2,1)}), bf16[64,4,1408]{2,1,0:T(4,128)(2,1)S(1)}, u32[]{:S(2)}, u32[]{:S(2)}) %all-to-all-start.2) | async-done | bytes 720928 | tf_op jit(solution)/shard_map/all_to_all | solution.py:329
  111.4 1.1 shard_map.118
  112.6 5.7 %all-to-all-start.3 = ((bf16[12,2,1408]{2,1,0:T(2,128)(2,1)}), bf16[12,2,1408]{2,1,0:T(2,128)(2,1)S(1)}, u32[]{:S(2)}, u32[]{:S(2)}) async-start(bf16[12,2,1408]{2,1,0:T(2,128)(2,1)} %shard_map.118), calls=%async_computation.3 | async-start | bytes 135168 | tf_op jit(solution)/shard_map/all_to_all | solution.py:353
  118.2 2.9 %fusion = bf16[1,4096,64]{1,2,0:T(8,128)(2,1)} fusion(bf16[256,4096]{1,0:T(8,128)(2,1)} %reshape_squeeze.3, bf16[128,256]{1,0:T(8,128)(2,1)S(1)} %get-tuple-element.54), kind=kOutput, calls=%fused_computation.2 | convolution fusion | flops 134479872 | bytes 2654208 | tf_op jit(solution)/shard_map/dot_general | solution.py:336
  121.1 0.0 collective-permute-done.4.low_ref
  121.1 0.0 collective-permute-done.5.high_ref
  121.1 0.9 shard_map.120
  122.0 7.4 %all-to-all-done.3.got_ref = bf16[12,2,1408]{2,1,0:T(2,128)(2,1)S(1)} async-done(((bf16[12,2,1408]{2,1,0:T(2,128)(2,1)}), bf16[12,2,1408]{2,1,0:T(2,128)(2,1)S(1)}, u32[]{:S(2)}, u32[]{:S(2)}) %all-to-all-start.3) | async-done | bytes 67616 | tf_op jit(solution)/shard_map/all_to_all | solution.py:353
  129.4 0.6 shard_map.119
  (1 shorter events, 0.0 us)
Async XLA Ops:
  0.6 0.7 copy-start.7
  2.0 26.3 %all-to-all-start = ((bf16[12,2,1408]{2,1,0:T(2,128)(2,1)}), bf16[12,2,1408]{2,1,0:T(2,128)(2,1)S(1)}, u32[]{:S(2)}, u32[]{:S(2)}) async-start(bf16[12,2,1408]{2,1,0:T(2,128)(2,1)} %shard_map.111), calls=%async_computation | async-start | bytes 135168 | tf_op jit(solution)/shard_map/all_to_all | solution.py:270
  17.2 1.0 copy-start
  18.2 1.0 copy-start.2
  19.3 1.0 copy-start.4
  21.4 0.7 copy-start.5
  22.1 0.7 copy-start.8
  29.5 32.4 %all-to-all-start.1 = ((bf16[64,4,1408]{2,1,0:T(4,128)(2,1)}), bf16[64,4,1408]{2,1,0:T(4,128)(2,1)S(1)}, u32[]{:S(2)}, u32[]{:S(2)}) async-start(bf16[64,4,1408]{2,1,0:T(4,128)(2,1)} %shard_map.113), calls=%async_computation.1 | async-start | bytes 1441792 | tf_op jit(solution)/shard_map/all_to_all | solution.py:300
  40.2 17.6 %copy-start.1 = (bf16[1,4096,64]{1,2,0:T(8,128)(2,1)S(1)}, bf16[1,4096,64]{1,2,0:T(8,128)(2,1)}, u32[]{:S(2)}) copy-start(bf16[1,4096,64]{1,2,0:T(8,128)(2,1)} %param.11) | copy-start | bytes 1572868
  40.2 21.0 %collective-permute-start = (bf16[64,1408]{1,0:T(8,128)(2,1)S(1)}, bf16[64,1408]{1,0:T(8,128)(2,1)S(1)}, u32[]{:S(2)}, u32[]{:S(2)}) collective-permute-start(bf16[64,1408]{1,0:T(8,128)(2,1)S(1)} %get-tuple-element.47), channel_id=1, source_target_pairs={{0,1},{1,2},{2,0},{3,4},{4,5},{5,3},{6,7},{7,8},{8,6},{9,10},{10,1... | collective-permute-start | bytes 540680 | tf_op jit(solution)/shard_map/ppermute | solution.py:264
  42.8 18.4 %collective-permute-start.1 = (bf16[64,1408]{1,0:T(8,128)(2,1)S(1)}, bf16[64,1408]{1,0:T(8,128)(2,1)S(1)}, u32[]{:S(2)}, u32[]{:S(2)}) collective-permute-start(bf16[64,1408]{1,0:T(8,128)(2,1)S(1)} %get-tuple-element.48), channel_id=1, source_target_pairs={{1,0},{2,1},{0,2},{4,3},{5,4},{3,5},{7,6},{8,7},{6,8},{10,9},{11,1... | collective-permute-start | bytes 540680 | tf_op jit(solution)/shard_map/ppermute | solution.py:264
  47.1 30.7 %collective-permute-start.2 = (bf16[128,1408]{1,0:T(8,128)(2,1)}, bf16[128,1408]{1,0:T(8,128)(2,1)S(1)}, u32[]{:S(2)}, u32[]{:S(2)}) collective-permute-start(bf16[128,1408]{1,0:T(8,128)(2,1)} %get-tuple-element.51), channel_id=1, source_target_pairs={{0,1},{1,2},{2,0},{3,4},{4,5},{5,3},{6,7},{7,8},{8,6},{9,10},{10,1... | collective-permute-start | bytes 1081352 | tf_op jit(solution)/shard_map/ppermute | solution.py:264
  49.0 28.8 %collective-permute-start.3 = (bf16[128,1408]{1,0:T(8,128)(2,1)}, bf16[128,1408]{1,0:T(8,128)(2,1)S(1)}, u32[]{:S(2)}, u32[]{:S(2)}) collective-permute-start(bf16[128,1408]{1,0:T(8,128)(2,1)} %get-tuple-element.52), channel_id=1, source_target_pairs={{1,0},{2,1},{0,2},{4,3},{5,4},{3,5},{7,6},{8,7},{6,8},{10,9},{11,1... | collective-permute-start | bytes 1081352 | tf_op jit(solution)/shard_map/ppermute | solution.py:264
  57.8 2.5 %copy-start.3 = (bf16[1,4096,64]{1,2,0:T(8,128)(2,1)S(1)}, bf16[1,4096,64]{1,2,0:T(8,128)(2,1)}, u32[]{:S(2)}) copy-start(bf16[1,4096,64]{1,2,0:T(8,128)(2,1)} %param.12) | copy-start | bytes 1572868
  57.8 2.5 %copy-start.9 = (bf16[256,4096]{1,0:T(8,128)(2,1)S(1)}, bf16[256,4096]{1,0:T(8,128)(2,1)}, u32[]{:S(2)}) copy-start(bf16[256,4096]{1,0:T(8,128)(2,1)} %reshape_squeeze.3) | copy-start | bytes 6291460
  62.7 26.9 %copy-start.6 = (s32[1,24,8]{1,2,0:T(8,128)S(1)}, s32[1,24,8]{1,2,0:T(8,128)}, u32[]{:S(2)}) copy-start(s32[1,24,8]{1,2,0:T(8,128)} %param.9) | copy-start | bytes 2308
  79.3 32.1 %all-to-all-start.2 = ((bf16[64,4,1408]{2,1,0:T(4,128)(2,1)}), bf16[64,4,1408]{2,1,0:T(4,128)(2,1)S(1)}, u32[]{:S(2)}, u32[]{:S(2)}) async-start(bf16[64,4,1408]{2,1,0:T(4,128)(2,1)} %get-tuple-element.53), calls=%async_computation.2 | async-start | bytes 1441792 | tf_op jit(solution)/shard_map/all_to_all | solution.py:329
  90.1 31.0 %collective-permute-start.4 = (bf16[64,1408]{1,0:T(8,128)(2,1)S(1)}, bf16[64,1408]{1,0:T(8,128)(2,1)S(1)}, u32[]{:S(2)}, u32[]{:S(2)}) collective-permute-start(bf16[64,1408]{1,0:T(8,128)(2,1)S(1)} %get-tuple-element.63), channel_id=1, source_target_pairs={{0,1},{1,2},{2,0},{3,4},{4,5},{5,3},{6,7},{7,8},{8,6},{9,10},{10,1... | collective-permute-start | bytes 540680 | tf_op jit(solution)/shard_map/ppermute | solution.py:264
  92.6 28.5 %collective-permute-start.5 = (bf16[64,1408]{1,0:T(8,128)(2,1)S(1)}, bf16[64,1408]{1,0:T(8,128)(2,1)S(1)}, u32[]{:S(2)}, u32[]{:S(2)}) collective-permute-start(bf16[64,1408]{1,0:T(8,128)(2,1)S(1)} %get-tuple-element.64), channel_id=1, source_target_pairs={{1,0},{2,1},{0,2},{4,3},{5,4},{3,5},{7,6},{8,7},{6,8},{10,9},{11,1... | collective-permute-start | bytes 540680 | tf_op jit(solution)/shard_map/ppermute | solution.py:264
  112.6 16.8 %all-to-all-start.3 = ((bf16[12,2,1408]{2,1,0:T(2,128)(2,1)}), bf16[12,2,1408]{2,1,0:T(2,128)(2,1)S(1)}, u32[]{:S(2)}, u32[]{:S(2)}) async-start(bf16[12,2,1408]{2,1,0:T(2,128)(2,1)} %shard_map.118), calls=%async_computation.3 | async-start | bytes 135168 | tf_op jit(solution)/shard_map/all_to_all | solution.py:353
